TPU v7x, 32 devices: a whole 2x2x4 slice. The times are simulated.
32 devices in a mesh: groups: 2 (over x), gy: 16 (over z, y, core).
Axes of the slice: x: 2, y: 2, z: 4, core: 2. Of those that a mesh axis runs over, the one named last changes fastest.
Arguments:
- observed: float32 [2048, 16, 256], P(('groups', 'gy')), parts along dimension 0, may hold values from -6 to 6
- tf_table: float32 [16], replicated, may hold values from 0.2 to 2
- tilt_index: int32 [513, 129], replicated, may hold values from 0 to 15
- wedge: int32 [513, 129], replicated, may hold values 0 or 1
Outputs:
- restored: float32 [2048, 16, 256], P(('groups', 'gy')), parts along dimension 0
There are 2 independent parts, one for each index of `groups`. A program takes and returns all parts, laid end to end along the dimension named above; an argument that names none is the same for every part. Nothing has to cross between parts.
All inputs are finite; a program needn't handle non-finite values.
Results may differ from a plain program's by a relative error of at most 0.00011.
Values sent between devices are 32-bit elements; how exact they have to be, the bound alone decides.
No kernel may reach another device: no remote copies, remote signals or barrier semaphores. Data moves between devices by JAX's collectives and lax.ppermute only.
A program may use at most 64 MiB of HBM per device.

v0:
```python
import functools

import jax
import jax.numpy as jnp
import ml_dtypes
import numpy as np
from jax import lax
from jax.experimental import pallas as pl
from jax.experimental.pallas import tpu as pltpu
from jax.sharding import PartitionSpec as P

OUTER = 2
PASSES = 2

step_dual = 0.14
step_primal = 0.14
huber_eps = 0.05
bound_dual = 0.5

SUB = 8
LANE = 128
HALO_LAST = 2 * PASSES
HALO_FIRST = HALO_LAST + 2 * PASSES - 2
UNROLL = 4
MIB = 1024 * 1024
MOST_VMEM = 62 * MIB

f32 = jnp.float32
bf16 = jnp.bfloat16

UNIT = step_dual / bound_dual


def halves(table):
    high = table.astype(ml_dtypes.bfloat16)
    low = (table - high.astype(np.float64)).astype(ml_dtypes.bfloat16)
    return np.stack([high, low])


def cas(rows, columns, length):
    phase = (rows[:, None] * columns[None, :]) % length
    angle = phase * (2.0 * np.pi / length)
    return np.cos(angle) + np.sin(angle)


def z_table(length):
    index = np.arange(length)
    return halves(cas(index, index, length))


def x_tables(length):
    half, quarter = length // 2, length // 4
    place = np.arange(half)
    fourth = cas(4 * place[:quarter], place[:quarter], length)
    second = cas(4 * place[:quarter] + 2, place[:quarter], length)
    odd = cas(2 * place + 1, place, length)
    small = np.stack([halves(fourth), halves(second), halves(second.T)])
    return small, np.stack([halves(odd), halves(odd.T)])


def kx_rows(length):
    half, quarter = length // 2, length // 4
    return ((0, quarter, 4, 0), (quarter, quarter, 4, 2), (half, half, 2, 1))


def padded_to(length, unit):
    return -(-length // unit) * unit


def weights_kernel(nx, nz, levels, table_ref, code_ref, data, prior):
    heights, widths = code_ref.shape
    scale = 1.0 / (nx * nz)
    kz = lax.broadcasted_iota(jnp.int32, (heights, nz), 1)
    kz = jnp.minimum(kz, nz - kz)
    pick_z = jnp.where(kz == lax.broadcasted_iota(jnp.int32, (heights, nz), 0), 1.0, 0.0)
    pick_z = pick_z.astype(bf16)
    for base, count, step, least in kx_rows(nx):
        tile = min(256, count)
        for top in range(0, count, tile):
            kx = step * (top + lax.broadcasted_iota(jnp.int32, (tile, widths), 0)) + least
            kx = jnp.minimum(kx, nx - kx)
            pick_x = jnp.where(kx == lax.broadcasted_iota(jnp.int32, (tile, widths), 1), 1.0, 0.0)
            tall = lax.dot_general(
                pick_x.astype(bf16),
                code_ref[...],
                (((1,), (1,)), ((), ())),
                preferred_element_type=f32,
            )
            spread = jnp.dot(tall.astype(bf16), pick_z, preferred_element_type=f32)
            response = jnp.zeros_like(spread)
            for level in range(levels):
                response = jnp.where(spread == level + 1.0, table_ref[level], response)
            gain = scale / (response * response + 1.0)
            rows = slice(base + top, base + top + tile)
            prior[rows] = gain
            data[rows] = (UNIT * response) * gain


def make_weights(tf_table, tilt_index, wedge, nx, nz):
    levels = tf_table.shape[0]
    code = jnp.where(wedge > 0, tilt_index + 1, 0).T
    extra = [(0, padded_to(size, LANE) - size) for size in code.shape]
    code = jnp.pad(code, extra).astype(bf16)
    grid = jax.ShapeDtypeStruct((nx, nz), f32)
    vmem = pl.BlockSpec(memory_space=pltpu.VMEM)
    return pl.pallas_call(
        functools.partial(weights_kernel, nx, nz, levels),
        in_specs=[pl.BlockSpec(memory_space=pltpu.SMEM), vmem],
        out_specs=[vmem] * 2,
        out_shape=[grid] * 2,
        compiler_params=pltpu.CompilerParams(vmem_limit_bytes=MOST_VMEM),
        cost_estimate=pl.CostEstimate(
            flops=60 * nx * nz, bytes_accessed=12 * nx * nz, transcendentals=0
        ),
    )(tf_table, code)


def split(value):
    high = value.astype(bf16)
    return high, (value - high.astype(f32)).astype(bf16)


def dot3(a, b):
    dot = functools.partial(jnp.dot, preferred_element_type=f32)
    return dot(a[0], b[0]) + (dot(a[0], b[1]) + dot(a[1], b[0]))


def turn_kernel(ny, planes, cells, turned, staged, placed, semaphores):
    blocks = len(staged)
    steps = placed.shape[1] // planes
    rows = planes * ny
    incoming = [
        [
            pltpu.make_async_copy(
                cells.at[pl.ds(step * rows, rows), pl.ds(LANE * k, LANE)],
                staged[k].at[pl.ds(step * rows, rows), :],
                semaphores.at[0, step, k],
            )
            for k in range(blocks)
        ]
        for step in range(steps)
    ]
    outgoing = [
        pltpu.make_async_copy(
            placed.at[:, pl.ds(step * planes, planes), :],
            turned.at[:, pl.ds(step * planes, planes), :],
            semaphores.at[1, step, 0],
        )
        for step in range(steps)
    ]
    for step in range(steps):
        for copy in incoming[step]:
            copy.start()
    for step in range(steps):
        for copy in incoming[step]:
            copy.wait()
        for y in range(ny):
            for x in range(step * planes, (step + 1) * planes, SUB):
                for k in range(blocks):
                    placed[y, x : x + SUB, LANE * k : LANE * (k + 1)] = staged[k][
                        pl.ds(x * ny + y, SUB, stride=ny), :
                    ]
        outgoing[step].start()
    for copy in outgoing:
        copy.wait()


def turn(observed):
    slab, ny, nz = observed.shape
    planes = 2 * SUB if slab % (2 * SUB) == 0 else SUB
    anywhere = pl.BlockSpec(memory_space=pltpu.HBM)
    return pl.pallas_call(
        functools.partial(turn_kernel, ny, planes),
        in_specs=[anywhere],
        out_specs=anywhere,
        out_shape=jax.ShapeDtypeStruct((ny, slab, nz), f32),
        scratch_shapes=[
            [pltpu.VMEM((slab * ny, LANE), f32)] * (nz // LANE),
            pltpu.VMEM((ny, slab, nz), f32),
            pltpu.SemaphoreType.DMA((2, slab // planes, nz // LANE)),
        ],
        compiler_params=pltpu.CompilerParams(vmem_limit_bytes=MOST_VMEM),
        cost_estimate=pl.CostEstimate(
            flops=0, bytes_accessed=8 * slab * ny * nz, transcendentals=0
        ),
    )(observed.reshape(slab * ny, nz))


def window_tiles(width, nz):
    return width * nz // (SUB * LANE)


def filter_kernel(first, halo, slab, *refs):
    cells, ztab_far, small_far, odd_far, refs = refs[0], refs[1], refs[2], refs[3], refs[4:]
    if first:
        data_far, prior_far, windows_far, kept_far, refs = refs[0], refs[1], refs[2], refs[3], refs[4:]
    else:
        kept_far, prior_far, windows, refs = refs[0], refs[1], refs[2], refs[3:]
    ztab, small, odd, scale, other, high, low, padded, semaphores, refs = refs[:9] + (refs[9:],)
    if first:
        windows, window_semaphores, cells_near = refs
        cells_copy = pltpu.make_async_copy(cells, cells_near, semaphores.at[7])
        cells_copy.start()
        cells = cells_near
    devices, rows, _, nz = cells.shape
    nx = devices * slab
    half, quarter = nx // 2, nx // 4
    width = slab + 2 * halo
    blocks = nz // LANE
    arrivals = [
        pltpu.make_async_copy(ztab_far, ztab, semaphores.at[0]),
        pltpu.make_async_copy(small_far, small, semaphores.at[1]),
        pltpu.make_async_copy(odd_far.at[0], odd.at[0], semaphores.at[2]),
        pltpu.make_async_copy(prior_far, scale, semaphores.at[3]),
    ]
    if first:
        arrivals.append(pltpu.make_async_copy(data_far, other.at[0], semaphores.at[4]))
    last_arrival = pltpu.make_async_copy(odd_far.at[1], odd.at[1], semaphores.at[5])
    for copy in arrivals:
        copy.start()

    def table(ref, i, rows=slice(None)):
        return ref[i, 0, rows], ref[i, 1, rows]

    def store(spot, value):
        high[spot], low[spot] = split(value)

    def load(spot):
        return high[spot], low[spot]

    parts = [slice(i * quarter, (i + 1) * quarter) for i in range(4)]
    folds = [parts[0], parts[1], slice(half, nx)]
    for r in range(rows):
        if not first:
            kept_copy = pltpu.make_async_copy(kept_far.at[r], other.at[0], semaphores.at[4])
            kept_copy.start()
        if r == 0:
            last_arrival.start()
        if first and r == 0:
            cells_copy.wait()
        q = [
            cells[i * devices // 4 : (i + 1) * devices // 4, r].reshape(quarter, nz)
            for i in range(4)
        ]
        even = (q[0] + q[2], q[1] + q[3])
        folded = (even[0] + even[1], even[0] - even[1], q[0] - q[2], q[1] - q[3])
        if r == 0:
            arrivals[0].wait()
        ztable = (ztab[0], ztab[1])
        for spot, value in zip(parts, folded):
            store(spot, dot3(split(value), ztable))
        if r == 0:
            arrivals[1].wait()
        waves = [dot3(table(small, i), load(folds[i])) for i in range(2)]
        if r == 0:
            arrivals[2].wait()
        for i in range(2):
            waves.append(dot3(table(odd, 0, parts[i]), load(folds[2])))
        if r == 0:
            for copy in arrivals[3:]:
                copy.wait()
        if not first:
            kept_copy.wait()
        for spot, wave in zip(parts, waves):
            if first:
                seen = wave * other[0, spot]
                other[1, spot] = seen
                store(spot, seen + wave * (UNIT * scale[spot]))
            else:
                store(spot, other[0, spot] + wave * scale[spot])
        if first:
            kept_copy = pltpu.make_async_copy(other.at[1], kept_far.at[r], semaphores.at[6])
            kept_copy.start()
        after = (halo + nx) // SUB * SUB
        padded[:SUB] = jnp.zeros((SUB, nz), f32)
        padded[after : after + 2 * SUB] = jnp.zeros((2 * SUB, nz), f32)
        plus, minus = dot3(table(small, 0), load(folds[0])), dot3(table(small, 2), load(folds[1]))
        if r == 0:
            last_arrival.wait()
        leaving = []
        written, sent = set(), set()
        for i, e in enumerate((plus + minus, plus - minus)):
            o = dot3(table(odd, 1, parts[i]), load(folds[2]))
            for j, value in ((i, e + o), (i + 2, e - o)):
                place = halo + j * quarter
                padded[place : place + quarter] = dot3(split(value), ztable)
                written |= set(range(j * quarter, (j + 1) * quarter))
            for device in range(devices):
                needed = range(device * slab - halo, (device + 1) * slab + halo)
                if device in sent or not written.issuperset(x for x in needed if 0 <= x < nx):
                    continue
                sent.add(device)
                for g in range(width // SUB):
                    spot = device * slab + SUB * g
                    for k in range(blocks):
                        windows[device, r, g * blocks + k] = padded[
                            spot : spot + SUB, LANE * k : LANE * (k + 1)
                        ]
                rest = width % SUB
                spot = device * slab + width - rest
                for k in range(blocks if rest else 0):
                    tile, row = width // SUB * blocks + k * rest // SUB, k * rest % SUB
                    windows[device, r, tile, row : row + rest] = padded[
                        spot : spot + rest, LANE * k : LANE * (k + 1)
                    ]
                if first:
                    copy = pltpu.make_async_copy(
                        windows.at[device, r], windows_far.at[device, r], window_semaphores.at[device]
                    )
                    copy.start()
                    leaving.append(copy)
        if first:
            for copy in leaving:
                copy.wait()
            kept_copy.wait()


def run_filter(first, halo, cells, tables, far):
    devices, rows, slab, nz = cells.shape
    nx = devices * slab
    ztab, small, odd = tables
    vmem = pl.BlockSpec(memory_space=pltpu.VMEM)
    hbm = pl.BlockSpec(memory_space=pltpu.HBM)
    windows = (devices, rows, window_tiles(slab + 2 * halo, nz), SUB, LANE)
    out_shape, out_specs = [jax.ShapeDtypeStruct(windows, f32)], [hbm if first else vmem]
    if first:
        out_shape.append(jax.ShapeDtypeStruct((rows, nx, nz), f32))
        out_specs.append(hbm)
    scratch_shapes = [
        pltpu.VMEM(ztab.shape, bf16),
        pltpu.VMEM(small.shape, bf16),
        pltpu.VMEM(odd.shape, bf16),
        pltpu.VMEM((nx, nz), f32),
        pltpu.VMEM((2, nx, nz), f32),
        pltpu.VMEM((nx, nz), bf16),
        pltpu.VMEM((nx, nz), bf16),
        pltpu.VMEM((nx + 3 * SUB, nz), f32),
        pltpu.SemaphoreType.DMA((8,)),
    ]
    if first:
        scratch_shapes += [
            pltpu.VMEM(windows, f32),
            pltpu.SemaphoreType.DMA((devices,)),
            pltpu.VMEM(cells.shape, f32),
        ]
    return pl.pallas_call(
        functools.partial(filter_kernel, first, halo, slab),
        in_specs=[hbm if first else vmem] + [hbm] * (3 + len(far)),
        out_specs=out_specs,
        out_shape=out_shape,
        scratch_shapes=scratch_shapes,
        compiler_params=pltpu.CompilerParams(
            vmem_limit_bytes=MOST_VMEM if first else 32 * MIB
        ),
        cost_estimate=pl.CostEstimate(
            flops=6 * rows * nx * nz * (2 * nz + nx),
            bytes_accessed=8 * rows * nx * nz,
            transcendentals=0,
        ),
    )(cells, ztab, small, odd, *far)


def lane_sums(pieces):
    lane = lax.broadcasted_iota(jnp.int32, pieces[0].shape, 1)
    up = [pltpu.roll(piece, LANE - 1, 1) for piece in pieces]
    down = [pltpu.roll(piece, 1, 1) for piece in pieces]
    sums = []
    for k in range(len(pieces)):
        above = up[k + 1] if k + 1 < len(pieces) else 0.0
        below = down[k - 1] if k > 0 else 0.0
        sums.append(
            jnp.where(lane == LANE - 1, above, up[k]) + jnp.where(lane == 0, below, down[k])
        )
    return sums


def row_sums(groups):
    row = lax.broadcasted_iota(jnp.int32, groups[0].shape, 0)
    up = [pltpu.roll(group, SUB - 1, 0) for group in groups]
    down = [pltpu.roll(group, 1, 0) for group in groups]
    count = len(groups)
    return [
        jnp.where(row == SUB - 1, up[(g + 1) % count], up[g])
        + jnp.where(row == 0, down[g - 1], down[g])
        for g in range(count)
    ]


def passes_kernel(first, last, halo, slab, nx, start_ref, target, *refs):
    if first:
        duals_in, refs = None, refs
    else:
        duals_in, refs = refs[:3], refs[3:]
    if last:
        restored, refs = refs[0], refs[1:]
    else:
        current, duals_out, refs = refs[0], refs[1:4], refs[4:]
    lead, field, dual_x, dual_y, dual_z = refs[:5]
    turned = refs[5:-1] if last else ()
    ny, _, nz = field.shape
    width = slab + 2 * halo
    groups = padded_to(width, SUB) // SUB
    blocks = nz // LANE
    decay = 1.0 / (1.0 + step_dual * huber_eps / bound_dual)
    gain = step_dual * decay
    floor = 1.0 / (decay * decay)
    keep = 1.0 / (1.0 + step_primal)
    pull = step_primal * keep
    push = pull * gain / decay
    origin = start_ref[0] - halo

    def goal_of(y, g, k):
        if SUB * (g + 1) <= width:
            return target[y, g * blocks + k]
        rest = width % SUB
        tail = target[y, g * blocks + k * rest // SUB]
        shift = k * rest % SUB
        return pltpu.roll(tail, SUB - shift, 0) if shift else tail

    def masked(value, g):
        if SUB * g >= halo and SUB * (g + 1) <= width - halo:
            return value
        place = origin + SUB * g + lax.broadcasted_iota(jnp.int32, (SUB, LANE), 0)
        return jnp.where((place >= 0) & (place < nx), value, 0.0)

    def at(g, k):
        return pl.ds(SUB * g, SUB), pl.ds(LANE * k, LANE)

    empty = jnp.zeros(lead.shape[1:], f32)
    for plane in (0, ny + 1):
        lead[plane] = empty
        dual_y[plane] = empty

    @pl.loop(0, ny, unroll=UNROLL)
    def _(y):
        for g in range(groups):
            for k in range(blocks):
                lead[(y + 1,) + at(g, k)] = goal_of(y, g, k)

    for sweep in range(PASSES):
        final = sweep == PASSES - 1

        @pl.loop(0, ny, unroll=UNROLL)
        def _(y):
            here = [[lead[(y + 1,) + at(g, k)] for k in range(blocks)] for g in range(groups)]
            columns = [row_sums([here[g][k] for g in range(groups)]) for k in range(blocks)]
            for g in range(groups):
                along_z = lane_sums(here[g])
                for k in range(blocks):
                    spot = at(g, k)
                    twice = here[g][k] + here[g][k]
                    along_y = lead[(y,) + spot] + lead[(y + 2,) + spot]
                    raised = [columns[k][g] - twice, along_y - twice, along_z[k] - twice]
                    if sweep > 0:
                        before = [dual_x[(y,) + spot], dual_y[(y + 1,) + spot], dual_z[(y,) + spot]]
                    elif duals_in is not None:
                        before = [ref[(y,) + spot] for ref in duals_in]
                    else:
                        before = None
                    if before is not None:
                        raised = [old + new for old, new in zip(before, raised)]
                    total = (
                        raised[0] * raised[0] + raised[1] * raised[1] + raised[2] * raised[2]
                    )
                    shrink = lax.rsqrt(jnp.maximum(floor, total))
                    made = [raised[0] * masked(shrink, g), raised[1] * shrink, raised[2] * shrink]
                    dual_x[(y,) + spot] = made[0]
                    dual_y[(y + 1,) + spot] = made[1]
                    dual_z[(y,) + spot] = made[2]
                    if final and not last:
                        shift = halo - HALO_LAST
                        lo = max(0, shift - SUB * g)
                        hi = min(SUB, slab + 2 * HALO_LAST + shift - SUB * g)
                        if lo < hi:
                            rows = pl.ds(SUB * g + lo - shift, hi - lo)
                            for a in range(3):
                                duals_out[a][y, rows, spot[1]] = made[a][lo:hi]

        @pl.loop(0, ny, unroll=UNROLL)
        def _(y):
            wanted = range(groups)
            if final:
                wanted = [
                    g for g in wanted if SUB * (g + 1) > halo and SUB * g < width - halo
                ]
            near = [[dual_x[(y,) + at(g, k)] for k in range(blocks)] for g in range(groups)]
            columns = [row_sums([near[g][k] for g in range(groups)]) for k in range(blocks)]
            for g in wanted:
                here = [dual_z[(y,) + at(g, k)] for k in range(blocks)]
                along_z = lane_sums(here)
                for k in range(blocks):
                    spot = at(g, k)
                    along_y = dual_y[(y,) + spot] + dual_y[(y + 2,) + spot]
                    centre = near[g][k] + dual_y[(y + 1,) + spot] + here[k]
                    adjoint = columns[k][g] + along_y + along_z[k] - (centre + centre)
                    goal = goal_of(y, g, k)
                    if sweep == 0:
                        move = push * adjoint
                        updated = goal - move
                        ahead = updated - move
                    else:
                        old = field[(y,) + spot]
                        whole = UNIT if final and last else 1.0
                        updated = (keep / whole) * old + (pull / whole) * goal
                        updated = updated - (push / whole) * adjoint
                        ahead = updated + updated - old
                    if not final:
                        field[(y,) + spot] = updated
                        lead[(y + 1,) + spot] = masked(ahead, g)
                        continue
                    lo = max(0, halo - SUB * g)
                    hi = min(SUB, slab + halo - SUB * g)
                    x = SUB * g + lo - halo
                    if last:
                        turned[k][pl.ds(x * ny + y, hi - lo, stride=ny), :] = updated[lo:hi]
                    else:
                        current[y, pl.ds(x, hi - lo), spot[1]] = updated[lo:hi]

    copies = [
        pltpu.make_async_copy(
            block, restored.at[:, pl.ds(LANE * k, LANE)], refs[-1].at[k]
        )
        for k, block in enumerate(turned)
    ]
    for copy in copies:
        copy.start()
    for copy in copies:
        copy.wait()


def run_passes(first, last, halo, slab, nx, start, target, duals):
    ny = target.shape[0]
    nz = target.shape[1] * SUB * LANE // (slab + 2 * halo)
    width = padded_to(slab + 2 * halo, SUB)
    vmem = pl.BlockSpec(memory_space=pltpu.VMEM)
    if last:
        out_shape = jax.ShapeDtypeStruct((slab * ny, nz), f32)
        out_specs = pl.BlockSpec(memory_space=pltpu.HBM)
    else:
        kept = jax.ShapeDtypeStruct((ny, slab + 2 * HALO_LAST, nz), f32)
        out_shape = [jax.ShapeDtypeStruct((ny, slab, nz), f32), kept, kept, kept]
        out_specs = [vmem] * 4
    return pl.pallas_call(
        functools.partial(passes_kernel, first, last, halo, slab, nx),
        in_specs=[pl.BlockSpec(memory_space=pltpu.SMEM)] + [vmem] * (1 + len(duals)),
        out_specs=out_specs,
        out_shape=out_shape,
        scratch_shapes=[
            pltpu.VMEM((ny + 2, width, nz), f32),
            pltpu.VMEM((ny, width, nz), f32),
            pltpu.VMEM((ny, width, nz), f32),
            pltpu.VMEM((ny + 2, width, nz), f32),
            pltpu.VMEM((ny, width, nz), f32),
        ]
        + [pltpu.VMEM((slab * ny, LANE), f32)] * (nz // LANE if last else 0)
        + [pltpu.SemaphoreType.DMA((nz // LANE,))] * last,
        compiler_params=pltpu.CompilerParams(vmem_limit_bytes=40 * MIB),
        cost_estimate=pl.CostEstimate(
            flops=60 * PASSES * ny * width * nz,
            bytes_accessed=8 * 4 * ny * width * nz,
            transcendentals=PASSES * ny * width * nz,
        ),
    )(start, target, *duals)


def exchange(blocks):
    return lax.all_to_all(blocks, "gy", split_axis=0, concat_axis=0, tiled=True)


def local(observed, tf_table, tilt_index, wedge):
    slab, ny, nz = observed.shape
    devices = lax.axis_size("gy")
    rows = ny // devices
    nx = slab * devices
    start = (lax.axis_index("gy") * slab).astype(jnp.int32).reshape(1)
    tables = [jnp.asarray(table) for table in (z_table(nz),) + x_tables(nx)]
    cells = exchange(turn(observed).reshape(devices, rows, slab, nz))
    data, prior = make_weights(tf_table, tilt_index, wedge, nx, nz)
    duals = ()
    for outer in range(OUTER):
        first, last = outer == 0, outer == OUTER - 1
        halo = HALO_LAST if last else HALO_FIRST
        made = run_filter(first, halo, cells, tables, (data, prior) if first else (kept, prior))
        if first:
            kept = made[1]
        windows = exchange(made[0])
        target = windows.reshape((ny,) + windows.shape[2:])
        made = run_passes(first, last, halo, slab, nx, start, target, duals)
        if last:
            return made.reshape(slab, ny, nz)
        duals = tuple(made[1:])
        cells = exchange(made[0].reshape(devices, rows, slab, nz))


def solution(mesh):
    in_specs = (P(("groups", "gy"), None, None), P(), P(), P())
    out_specs = P(("groups", "gy"), None, None)
    return jax.shard_map(local, mesh=mesh, in_specs=in_specs, out_specs=out_specs, check_vma=False)
```

profile of v0, /device:TPU:8, one launch (start us, length us, event | category | flops | bytes accessed | tf_op | source)
XLA Modules:
  0.0 151.8 jit_solution(5514972860366877560)
XLA Ops:
  0.0 2.2 %shard_map.73 = f32[16,64,256]{2,1,0:T(8,128)} custom-call(f32[1024,256]{1,0:T(8,128)} %bitcast.13), custom_call_target="tpu_custom_call" | custom-call | bytes 2097152 | tf_op jit(solution)/shard_map/pallas_call | solution.py:172
  2.2 0.0 copy-start.6
  2.2 0.0 copy-start.7
  2.2 6.4 %all-to-all-start = ((f32[16,1,64,256]{3,2,1,0:T(8,128)}), f32[16,1,64,256]{3,2,1,0:T(8,128)S(1)}, u32[]{:S(2)}, u32[]{:S(2)}) async-start(f32[16,1,64,256]{3,2,1,0:T(8,128)} %bitcast.12), calls=%async_computation | async-start | bytes 2097152 | tf_op jit(solution)/shard_map/all_to_all | solution.py:567
  8.7 0.0 copy-done.6
  8.7 0.0 copy-done.7
  8.7 0.1 fusion
  8.8 0.8 pad.5.code_ref
  9.5 4.7 %shard_map.74 = (f32[1024,256]{1,0:T(8,128)}, f32[1024,256]{1,0:T(8,128)}) custom-call(f32[16]{0:T(128)} %table_ref.1, bf16[256,640]{1,0:T(8,128)(2,1)} %pad.5.code_ref), custom_call_target="tpu_custom_call" | custom-call | flops 15728640 | bytes 3145728 | tf_op jit(solution)/shard_map/pallas_call | solution.py:106
  14.2 18.7 %all-to-all-done.refs_0_ = f32[16,1,64,256]{3,2,1,0:T(8,128)S(1)} async-done(((f32[16,1,64,256]{3,2,1,0:T(8,128)}), f32[16,1,64,256]{3,2,1,0:T(8,128)S(1)}, u32[]{:S(2)}, u32[]{:S(2)}) %all-to-all-start) | async-done | bytes 1048608 | tf_op jit(solution)/shard_map/all_to_all | solution.py:567
  32.9 0.0 copy-start.5
  32.9 1.0 copy-done.5
  33.9 5.8 %shard_map.75 = (f32[16,1,19,8,128]{4,3,2,1,0:T(8,128)}, f32[1,1024,256]{2,1,0:T(8,128)}) custom-call(f32[16,1,64,256]{3,2,1,0:T(8,128)} %copy-done.5, bf16[2,256,256]{2,1,0:T(8,128)(2,1)} %constant.19.clone.refs_1_, bf16[3,2,256,256]{3,2,1,0:T(8,128)(2,1)} %constant.20.clone.refs_2_, bf16[2,2,512,512]{3,2,1,0:T(8,128)(2,1)} %constant.21.clone.refs_3_, ...), custom_call_target="tpu_custom_call" | custom-call | flops 2415919104 | bytes 2097152 | tf_op jit(solution)/shard_map/pallas_call | solution.py:346
  39.7 0.0 copy-start.2
  39.7 0.0 copy-start.3
  39.8 0.0 copy-start.4
  39.8 5.7 %all-to-all-start.1 = ((f32[16,1,19,8,128]{4,3,2,1,0:T(8,128)}), f32[16,1,19,8,128]{4,3,2,1,0:T(8,128)S(1)}, u32[]{:S(2)}, u32[]{:S(2)}) async-start(f32[16,1,19,8,128]{4,3,2,1,0:T(8,128)} %get-tuple-element.15), calls=%async_computation.1 | async-start | bytes 2490368 | tf_op jit(solution)/shard_map/all_to_all | solution.py:567
  45.5 28.2 %all-to-all-done.1 = f32[16,1,19,8,128]{4,3,2,1,0:T(8,128)S(1)} async-done(((f32[16,1,19,8,128]{4,3,2,1,0:T(8,128)}), f32[16,1,19,8,128]{4,3,2,1,0:T(8,128)S(1)}, u32[]{:S(2)}, u32[]{:S(2)}) %all-to-all-start.1) | async-done | bytes 1245216 | tf_op jit(solution)/shard_map/all_to_all | solution.py:567
  73.8 0.0 copy-start.1
  73.8 4.6 %shard_map.76 = (f32[16,64,256]{2,1,0:T(8,128)S(1)}, f32[16,72,256]{2,1,0:T(8,128)S(1)}, f32[16,72,256]{2,1,0:T(8,128)S(1)}, f32[16,72,256]{2,1,0:T(8,128)S(1)}) custom-call(s32[1]{0:T(128)} %bitcast.start_ref, f32[16,19,8,128]{3,2,1,0:T(8,128)S(1)} %bitcast.9), custom_call_target="tpu_custom_call" | custom-call | flops 39321600 | bytes 10485760 | tf_op jit(solution)/shard_map/pallas_call | solution.py:543
  78.4 0.0 copy-start
  78.4 30.6 %all_to_all.20.refs_0_ = f32[16,1,64,256]{3,2,1,0:T(8,128)S(1)} all-to-all(f32[16,1,64,256]{3,2,1,0:T(8,128)S(1)} %bitcast.11), channel_id=1, replica_groups=mesh['groups'=2,'gy'=16] {'gy'}, dimensions={0} | all-to-all | bytes 2097152 | tf_op jit(solution)/shard_map/all_to_all | solution.py:567
  109.0 0.0 copy-done.2
  109.0 0.0 copy-done.3
  109.0 0.0 copy-done.4
  109.0 0.0 copy-done.1
  109.0 0.0 copy-done
  109.0 4.1 %shard_map.77 = f32[16,1,18,8,128]{4,3,2,1,0:T(8,128)S(1)} custom-call(f32[16,1,64,256]{3,2,1,0:T(8,128)S(1)} %all_to_all.20.refs_0_, bf16[2,256,256]{2,1,0:T(8,128)(2,1)S(1)} %copy-done.3, bf16[3,2,256,256]{3,2,1,0:T(8,128)(2,1)S(1)} %copy-done.2, bf16[2,2,512,512]{3,2,1,0:T(8,128)(2,1)S(1)} %copy-done.1, f32[1,1024,256]{2,1,0:T(8,128)S(1)} %copy-done.4, ...), custom_call_target="tpu_custom_call" | custom-call | flops 2415919104 | bytes 2097152 | tf_op jit(solution)/shard_map/pallas_call | solution.py:346
  113.2 33.2 %all_to_all.21 = f32[16,1,18,8,128]{4,3,2,1,0:T(8,128)S(1)} all-to-all(f32[16,1,18,8,128]{4,3,2,1,0:T(8,128)S(1)} %shard_map.77), channel_id=1, replica_groups=mesh['groups'=2,'gy'=16] {'gy'}, dimensions={0} | all-to-all | bytes 2359296 | tf_op jit(solution)/shard_map/all_to_all | solution.py:567
  146.4 5.4 %shard_map.78 = f32[1024,256]{1,0:T(8,128)} custom-call(s32[1]{0:T(128)} %bitcast.start_ref, f32[16,18,8,128]{3,2,1,0:T(8,128)S(1)} %bitcast.10, f32[16,72,256]{2,1,0:T(8,128)S(1)} %get-tuple-element.18.refs_0_, f32[16,72,256]{2,1,0:T(8,128)S(1)} %get-tuple-element.19.refs_1_, f32[16,72,256]{2,1,0:T(8,128)S(1)} %get-tuple-element.20.refs_2_), custom_call_target="tpu_custom_call" | custom-call | flops 35389440 | bytes 9437184 | tf_op jit(solution)/shard_map/pallas_call | solution.py:543
Async XLA Ops:
  2.2 6.5 %copy-start.6 = (s32[513,129]{0,1:T(8,128)S(1)}, s32[513,129]{0,1:T(8,128)}, u32[]{:S(2)}) copy-start(s32[513,129]{0,1:T(8,128)} %param.9) | copy-start | bytes 794128
  2.2 6.5 %copy-start.7 = (s32[513,129]{0,1:T(8,128)S(1)}, s32[513,129]{0,1:T(8,128)}, u32[]{:S(2)}) copy-start(s32[513,129]{0,1:T(8,128)} %param.10) | copy-start | bytes 794128
  2.2 30.7 %all-to-all-start = ((f32[16,1,64,256]{3,2,1,0:T(8,128)}), f32[16,1,64,256]{3,2,1,0:T(8,128)S(1)}, u32[]{:S(2)}, u32[]{:S(2)}) async-start(f32[16,1,64,256]{3,2,1,0:T(8,128)} %bitcast.12), calls=%async_computation | async-start | bytes 2097152 | tf_op jit(solution)/shard_map/all_to_all | solution.py:567
  32.9 1.0 copy-start.5
  39.7 69.3 %copy-start.2 = (bf16[3,2,256,256]{3,2,1,0:T(8,128)(2,1)S(1)}, bf16[3,2,256,256]{3,2,1,0:T(8,128)(2,1)}, u32[]{:S(2)}) copy-start(bf16[3,2,256,256]{3,2,1,0:T(8,128)(2,1)} %constant.20.clone.refs_2_) | copy-start | bytes 2359300
  39.7 69.3 %copy-start.3 = (bf16[2,256,256]{2,1,0:T(8,128)(2,1)S(1)}, bf16[2,256,256]{2,1,0:T(8,128)(2,1)}, u32[]{:S(2)}) copy-start(bf16[2,256,256]{2,1,0:T(8,128)(2,1)} %constant.19.clone.refs_1_) | copy-start | bytes 786436
  39.8 69.2 %copy-start.4 = (f32[1,1024,256]{2,1,0:T(8,128)S(1)}, f32[1,1024,256]{2,1,0:T(8,128)}, u32[]{:S(2)}) copy-start(f32[1,1024,256]{2,1,0:T(8,128)} %get-tuple-element.17.refs_4_) | copy-start | bytes 3145732
  39.8 34.0 %all-to-all-start.1 = ((f32[16,1,19,8,128]{4,3,2,1,0:T(8,128)}), f32[16,1,19,8,128]{4,3,2,1,0:T(8,128)S(1)}, u32[]{:S(2)}, u32[]{:S(2)}) async-start(f32[16,1,19,8,128]{4,3,2,1,0:T(8,128)} %get-tuple-element.15), calls=%async_computation.1 | async-start | bytes 2490368 | tf_op jit(solution)/shard_map/all_to_all | solution.py:567
  73.8 35.3 %copy-start.1 = (bf16[2,2,512,512]{3,2,1,0:T(8,128)(2,1)S(1)}, bf16[2,2,512,512]{3,2,1,0:T(8,128)(2,1)}, u32[]{:S(2)}) copy-start(bf16[2,2,512,512]{3,2,1,0:T(8,128)(2,1)} %constant.21.clone.refs_3_) | copy-start | bytes 6291460
  78.4 30.6 %copy-start = (f32[1024,256]{1,0:T(8,128)S(1)}, f32[1024,256]{1,0:T(8,128)}, u32[]{:S(2)}) copy-start(f32[1024,256]{1,0:T(8,128)} %get-tuple-element.14.refs_5_) | copy-start | bytes 3145732
where the time goes:
time: 154 us; the launch traced here: 152 us
  blocking collectives  63.8 us (41%)
  waiting for transfers between devices  47 us (31%)
  Pallas kernels  26.9 us (17%)
  starting transfers between devices  12.2 us (8%)
  local copies, waits for them, and re-layouts  1.76 us (1%)
    all_to_all x2, blocking collectives, exchange(): return lax.all_to_all(blocks, 'gy', split_axis=0, concat_axis=0, tiled=True)  63.8 us
    all_to_all x2, waiting for transfers between devices, exchange(): return lax.all_to_all(blocks, 'gy', split_axis=0, concat_axis=0, tiled=True)  47 us
    all_to_all x2, starting transfers between devices, exchange(): return lax.all_to_all(blocks, 'gy', split_axis=0, concat_axis=0, tiled=True)  12.2 us
    pallas_call x2, Pallas kernels, run_passes(): pl.pallas_call(functools.partial(passes_kernel, first, last, halo, slab,...  10.1 us
    pallas_call x2, Pallas kernels, run_filter(): pl.pallas_call(functools.partial(filter_kernel, first, halo, slab), in_sp...  9.98 us
    pallas_call x1, Pallas kernels, make_weights(): pl.pallas_call(functools.partial(weights_kernel, nx, nz, levels), in_spec...  4.66 us
  transfers between devices with their start and end apart: 2, of which 2 were waited for; matrix products, arithmetic and copies ran while one was open for 1% of the time, Pallas kernels for 3%

commit v1 on v0

--- a/solution.py
+++ b/solution.py
@@ -21,9 +21,10 @@
 LANE = 128
 HALO_LAST = 2 * PASSES
 HALO_FIRST = HALO_LAST + 2 * PASSES - 2
-UNROLL = 4
+UNROLL = 8
+COLUMN = 3
 MIB = 1024 * 1024
-MOST_VMEM = 62 * MIB
+MOST_VMEM = 61 * MIB
 
 f32 = jnp.float32
 bf16 = jnp.bfloat16
@@ -121,8 +122,9 @@
 
 
 def dot3(a, b):
-    dot = functools.partial(jnp.dot, preferred_element_type=f32)
-    return dot(a[0], b[0]) + (dot(a[0], b[1]) + dot(a[1], b[0]))
+    wide = jnp.concatenate([a[0], a[0], a[1]], axis=1)
+    tall = jnp.concatenate([b[0], b[1], b[0]], axis=0)
+    return jnp.dot(wide, tall, preferred_element_type=f32)
 
 
 def turn_kernel(ny, planes, cells, turned, staged, placed, semaphores):
@@ -198,10 +200,7 @@
         kept_far, prior_far, windows, refs = refs[0], refs[1], refs[2], refs[3:]
     ztab, small, odd, scale, other, high, low, padded, semaphores, refs = refs[:9] + (refs[9:],)
     if first:
-        windows, window_semaphores, cells_near = refs
-        cells_copy = pltpu.make_async_copy(cells, cells_near, semaphores.at[7])
-        cells_copy.start()
-        cells = cells_near
+        windows, window_semaphores = refs
     devices, rows, _, nz = cells.shape
     nx = devices * slab
     half, quarter = nx // 2, nx // 4
@@ -236,8 +235,6 @@
             kept_copy.start()
         if r == 0:
             last_arrival.start()
-        if first and r == 0:
-            cells_copy.wait()
         q = [
             cells[i * devices // 4 : (i + 1) * devices // 4, r].reshape(quarter, nz)
             for i in range(4)
@@ -335,17 +332,16 @@
         pltpu.VMEM((nx, nz), bf16),
         pltpu.VMEM((nx, nz), bf16),
         pltpu.VMEM((nx + 3 * SUB, nz), f32),
-        pltpu.SemaphoreType.DMA((8,)),
+        pltpu.SemaphoreType.DMA((7,)),
     ]
     if first:
         scratch_shapes += [
             pltpu.VMEM(windows, f32),
             pltpu.SemaphoreType.DMA((devices,)),
-            pltpu.VMEM(cells.shape, f32),
         ]
     return pl.pallas_call(
         functools.partial(filter_kernel, first, halo, slab),
-        in_specs=[hbm if first else vmem] + [hbm] * (3 + len(far)),
+        in_specs=[vmem] + [hbm] * (3 + len(far)),
         out_specs=out_specs,
         out_shape=out_shape,
         scratch_shapes=scratch_shapes,
@@ -375,14 +371,16 @@
 
 
 def row_sums(groups):
+    return inner_row_sums([groups[-1]] + groups + [groups[0]])
+
+
+def inner_row_sums(groups):
     row = lax.broadcasted_iota(jnp.int32, groups[0].shape, 0)
     up = [pltpu.roll(group, SUB - 1, 0) for group in groups]
     down = [pltpu.roll(group, 1, 0) for group in groups]
-    count = len(groups)
     return [
-        jnp.where(row == SUB - 1, up[(g + 1) % count], up[g])
-        + jnp.where(row == 0, down[g - 1], down[g])
-        for g in range(count)
+        jnp.where(row == SUB - 1, up[g + 1], up[g]) + jnp.where(row == 0, down[g - 1], down[g])
+        for g in range(1, len(groups) - 1)
     ]
 
 
@@ -437,6 +435,7 @@
             for k in range(blocks):
                 lead[(y + 1,) + at(g, k)] = goal_of(y, g, k)
 
+    leaving = []
     for sweep in range(PASSES):
         final = sweep == PASSES - 1
 
@@ -476,55 +475,63 @@
                             for a in range(3):
                                 duals_out[a][y, rows, spot[1]] = made[a][lo:hi]
 
-        @pl.loop(0, ny, unroll=UNROLL)
-        def _(y):
-            wanted = range(groups)
-            if final:
-                wanted = [
-                    g for g in wanted if SUB * (g + 1) > halo and SUB * g < width - halo
-                ]
-            near = [[dual_x[(y,) + at(g, k)] for k in range(blocks)] for g in range(groups)]
-            columns = [row_sums([near[g][k] for g in range(groups)]) for k in range(blocks)]
-            for g in wanted:
-                here = [dual_z[(y,) + at(g, k)] for k in range(blocks)]
-                along_z = lane_sums(here)
-                for k in range(blocks):
-                    spot = at(g, k)
-                    along_y = dual_y[(y,) + spot] + dual_y[(y + 2,) + spot]
-                    centre = near[g][k] + dual_y[(y + 1,) + spot] + here[k]
-                    adjoint = columns[k][g] + along_y + along_z[k] - (centre + centre)
-                    goal = goal_of(y, g, k)
-                    if sweep == 0:
-                        move = push * adjoint
-                        updated = goal - move
-                        ahead = updated - move
-                    else:
-                        old = field[(y,) + spot]
-                        whole = UNIT if final and last else 1.0
-                        updated = (keep / whole) * old + (pull / whole) * goal
-                        updated = updated - (push / whole) * adjoint
-                        ahead = updated + updated - old
-                    if not final:
-                        field[(y,) + spot] = updated
-                        lead[(y + 1,) + spot] = masked(ahead, g)
-                        continue
-                    lo = max(0, halo - SUB * g)
-                    hi = min(SUB, slab + halo - SUB * g)
-                    x = SUB * g + lo - halo
-                    if last:
-                        turned[k][pl.ds(x * ny + y, hi - lo, stride=ny), :] = updated[lo:hi]
-                    else:
-                        current[y, pl.ds(x, hi - lo), spot[1]] = updated[lo:hi]
-
-    copies = [
-        pltpu.make_async_copy(
-            block, restored.at[:, pl.ds(LANE * k, LANE)], refs[-1].at[k]
-        )
-        for k, block in enumerate(turned)
-    ]
-    for copy in copies:
-        copy.start()
-    for copy in copies:
+        wanted = list(range(groups))
+        if final:
+            wanted = [g for g in wanted if SUB * (g + 1) > halo and SUB * g < width - halo]
+        column = COLUMN if final and last else len(wanted)
+        for some in [wanted[i : i + column] for i in range(0, len(wanted), column)]:
+
+            @pl.loop(0, ny, unroll=UNROLL)
+            def _(y):
+                around = [some[0] - 1] + some + [some[-1] + 1]
+                near = {
+                    g: [dual_x[(y,) + at(g % groups, k)] for k in range(blocks)] for g in around
+                }
+                columns = [inner_row_sums([near[g][k] for g in around]) for k in range(blocks)]
+                for place, g in enumerate(some):
+                    here = [dual_z[(y,) + at(g, k)] for k in range(blocks)]
+                    along_z = lane_sums(here)
+                    for k in range(blocks):
+                        spot = at(g, k)
+                        along_y = dual_y[(y,) + spot] + dual_y[(y + 2,) + spot]
+                        centre = near[g][k] + dual_y[(y + 1,) + spot] + here[k]
+                        adjoint = columns[k][place] + along_y + along_z[k] - (centre + centre)
+                        goal = goal_of(y, g, k)
+                        if sweep == 0:
+                            move = push * adjoint
+                            updated = goal - move
+                            ahead = updated - move
+                        else:
+                            old = field[(y,) + spot]
+                            whole = UNIT if final and last else 1.0
+                            updated = (keep / whole) * old + (pull / whole) * goal
+                            updated = updated - (push / whole) * adjoint
+                            ahead = updated + updated - old
+                        if not final:
+                            field[(y,) + spot] = updated
+                            lead[(y + 1,) + spot] = masked(ahead, g)
+                            continue
+                        lo = max(0, halo - SUB * g)
+                        hi = min(SUB, slab + halo - SUB * g)
+                        x = SUB * g + lo - halo
+                        if last:
+                            turned[k][pl.ds(x * ny + y, hi - lo, stride=ny), :] = updated[lo:hi]
+                        else:
+                            current[y, pl.ds(x, hi - lo), spot[1]] = updated[lo:hi]
+
+            if final and last:
+                low = max(0, SUB * some[0] - halo) * ny
+                high = min(slab, SUB * (some[-1] + 1) - halo) * ny
+                for k, block in enumerate(turned):
+                    copy = pltpu.make_async_copy(
+                        block.at[pl.ds(low, high - low), :],
+                        restored.at[pl.ds(low, high - low), pl.ds(LANE * k, LANE)],
+                        refs[-1].at[len(leaving)],
+                    )
+                    copy.start()
+                    leaving.append(copy)
+
+    for copy in leaving:
         copy.wait()
 
 
@@ -553,7 +560,7 @@
             pltpu.VMEM((ny, width, nz), f32),
         ]
         + [pltpu.VMEM((slab * ny, LANE), f32)] * (nz // LANE if last else 0)
-        + [pltpu.SemaphoreType.DMA((nz // LANE,))] * last,
+        + [pltpu.SemaphoreType.DMA((nz // LANE * width // SUB,))] * last,
         compiler_params=pltpu.CompilerParams(vmem_limit_bytes=40 * MIB),
         cost_estimate=pl.CostEstimate(
             flops=60 * PASSES * ny * width * nz,

time: 154 us -> 155 us (level)
  no operation moved by 1% of the time
where the time goes in v1:
time: 155 us; the launch traced here: 152 us
  blocking collectives  63.8 us (41%)
  waiting for transfers between devices  47 us (30%)
  Pallas kernels  27.2 us (18%)
  starting transfers between devices  12.2 us (8%)
  local copies, waits for them, and re-layouts  1.76 us (1%)
    all_to_all x2, blocking collectives, exchange(): return lax.all_to_all(blocks, 'gy', split_axis=0, concat_axis=0, tiled=True)  63.8 us
    all_to_all x2, waiting for transfers between devices, exchange(): return lax.all_to_all(blocks, 'gy', split_axis=0, concat_axis=0, tiled=True)  47 us
    all_to_all x2, starting transfers between devices, exchange(): return lax.all_to_all(blocks, 'gy', split_axis=0, concat_axis=0, tiled=True)  12.2 us
    pallas_call x2, Pallas kernels, run_filter(): pl.pallas_call(functools.partial(filter_kernel, first, halo, slab), in_sp...  10.7 us
    pallas_call x2, Pallas kernels, run_passes(): pl.pallas_call(functools.partial(passes_kernel, first, last, halo, slab,...  9.63 us
    pallas_call x1, Pallas kernels, make_weights(): pl.pallas_call(functools.partial(weights_kernel, nx, nz, levels), in_spec...  4.66 us
  transfers between devices with their start and end apart: 2, of which 2 were waited for; matrix products, arithmetic and copies ran while one was open for 1% of the time, Pallas kernels for 3%

profile of v1, /device:TPU:8, one launch (start us, length us, event | category | flops | bytes accessed | tf_op | source)
XLA Modules:
  0.0 152.1 jit_solution(17198890533768348896)
XLA Ops:
  0.0 2.2 %shard_map.73 = f32[16,64,256]{2,1,0:T(8,128)} custom-call(f32[1024,256]{1,0:T(8,128)} %bitcast.13), custom_call_target="tpu_custom_call" | custom-call | bytes 2097152 | tf_op jit(solution)/shard_map/pallas_call | solution.py:174
  2.2 0.0 copy-start.6
  2.2 0.0 copy-start.7
  2.2 6.4 %all-to-all-start = ((f32[16,1,64,256]{3,2,1,0:T(8,128)}), f32[16,1,64,256]{3,2,1,0:T(8,128)S(1)}, u32[]{:S(2)}, u32[]{:S(2)}) async-start(f32[16,1,64,256]{3,2,1,0:T(8,128)} %bitcast.12), calls=%async_computation | async-start | bytes 2097152 | tf_op jit(solution)/shard_map/all_to_all | solution.py:574
  8.7 0.0 copy-done.6
  8.7 0.0 copy-done.7
  8.7 0.1 fusion
  8.8 0.8 pad.5.code_ref
  9.5 4.7 %shard_map.74 = (f32[1024,256]{1,0:T(8,128)}, f32[1024,256]{1,0:T(8,128)}) custom-call(f32[16]{0:T(128)} %table_ref.1, bf16[256,640]{1,0:T(8,128)(2,1)} %pad.5.code_ref), custom_call_target="tpu_custom_call" | custom-call | flops 15728640 | bytes 3145728 | tf_op jit(solution)/shard_map/pallas_call | solution.py:107
  14.2 18.7 %all-to-all-done.refs_0_ = f32[16,1,64,256]{3,2,1,0:T(8,128)S(1)} async-done(((f32[16,1,64,256]{3,2,1,0:T(8,128)}), f32[16,1,64,256]{3,2,1,0:T(8,128)S(1)}, u32[]{:S(2)}, u32[]{:S(2)}) %all-to-all-start) | async-done | bytes 1048608 | tf_op jit(solution)/shard_map/all_to_all | solution.py:574
  32.9 0.0 copy-start.5
  32.9 1.0 copy-done.5
  33.9 6.6 %shard_map.75 = (f32[16,1,19,8,128]{4,3,2,1,0:T(8,128)}, f32[1,1024,256]{2,1,0:T(8,128)}) custom-call(f32[16,1,64,256]{3,2,1,0:T(8,128)} %copy-done.5, bf16[2,256,256]{2,1,0:T(8,128)(2,1)} %constant.19.clone.refs_1_, bf16[3,2,256,256]{3,2,1,0:T(8,128)(2,1)} %constant.20.clone.refs_2_, bf16[2,2,512,512]{3,2,1,0:T(8,128)(2,1)} %constant.21.clone.refs_3_, ...), custom_call_target="tpu_custom_call" | custom-call | flops 2415919104 | bytes 2097152 | tf_op jit(solution)/shard_map/pallas_call | solution.py:342
  40.5 0.0 copy-start.2
  40.5 0.0 copy-start.3
  40.5 0.0 copy-start.4
  40.6 5.7 %all-to-all-start.1 = ((f32[16,1,19,8,128]{4,3,2,1,0:T(8,128)}), f32[16,1,19,8,128]{4,3,2,1,0:T(8,128)S(1)}, u32[]{:S(2)}, u32[]{:S(2)}) async-start(f32[16,1,19,8,128]{4,3,2,1,0:T(8,128)} %get-tuple-element.15), calls=%async_computation.1 | async-start | bytes 2490368 | tf_op jit(solution)/shard_map/all_to_all | solution.py:574
  46.3 28.2 %all-to-all-done.1 = f32[16,1,19,8,128]{4,3,2,1,0:T(8,128)S(1)} async-done(((f32[16,1,19,8,128]{4,3,2,1,0:T(8,128)}), f32[16,1,19,8,128]{4,3,2,1,0:T(8,128)S(1)}, u32[]{:S(2)}, u32[]{:S(2)}) %all-to-all-start.1) | async-done | bytes 1245216 | tf_op jit(solution)/shard_map/all_to_all | solution.py:574
  74.5 0.0 copy-start.1
  74.5 4.4 %shard_map.76 = (f32[16,64,256]{2,1,0:T(8,128)S(1)}, f32[16,72,256]{2,1,0:T(8,128)S(1)}, f32[16,72,256]{2,1,0:T(8,128)S(1)}, f32[16,72,256]{2,1,0:T(8,128)S(1)}) custom-call(s32[1]{0:T(128)} %bitcast.start_ref, f32[16,19,8,128]{3,2,1,0:T(8,128)S(1)} %bitcast.9), custom_call_target="tpu_custom_call" | custom-call | flops 39321600 | bytes 10485760 | tf_op jit(solution)/shard_map/pallas_call | solution.py:550
  78.9 0.0 copy-start
  78.9 30.6 %all_to_all.20.refs_0_ = f32[16,1,64,256]{3,2,1,0:T(8,128)S(1)} all-to-all(f32[16,1,64,256]{3,2,1,0:T(8,128)S(1)} %bitcast.11), channel_id=1, replica_groups=mesh['groups'=2,'gy'=16] {'gy'}, dimensions={0} | all-to-all | bytes 2097152 | tf_op jit(solution)/shard_map/all_to_all | solution.py:574
  109.5 0.0 copy-done.2
  109.5 0.0 copy-done.3
  109.5 0.0 copy-done.4
  109.5 0.0 copy-done.1
  109.5 0.0 copy-done
  109.5 4.1 %shard_map.77 = f32[16,1,18,8,128]{4,3,2,1,0:T(8,128)S(1)} custom-call(f32[16,1,64,256]{3,2,1,0:T(8,128)S(1)} %all_to_all.20.refs_0_, bf16[2,256,256]{2,1,0:T(8,128)(2,1)S(1)} %copy-done.3, bf16[3,2,256,256]{3,2,1,0:T(8,128)(2,1)S(1)} %copy-done.2, bf16[2,2,512,512]{3,2,1,0:T(8,128)(2,1)S(1)} %copy-done.1, f32[1,1024,256]{2,1,0:T(8,128)S(1)} %copy-done.4, ...), custom_call_target="tpu_custom_call" | custom-call | flops 2415919104 | bytes 2097152 | tf_op jit(solution)/shard_map/pallas_call | solution.py:342
  113.7 33.2 %all_to_all.21 = f32[16,1,18,8,128]{4,3,2,1,0:T(8,128)S(1)} all-to-all(f32[16,1,18,8,128]{4,3,2,1,0:T(8,128)S(1)} %shard_map.77), channel_id=1, replica_groups=mesh['groups'=2,'gy'=16] {'gy'}, dimensions={0} | all-to-all | bytes 2359296 | tf_op jit(solution)/shard_map/all_to_all | solution.py:574
  146.8 5.3 %shard_map.78 = f32[1024,256]{1,0:T(8,128)} custom-call(s32[1]{0:T(128)} %bitcast.start_ref, f32[16,18,8,128]{3,2,1,0:T(8,128)S(1)} %bitcast.10, f32[16,72,256]{2,1,0:T(8,128)S(1)} %get-tuple-element.18.refs_0_, f32[16,72,256]{2,1,0:T(8,128)S(1)} %get-tuple-element.19.refs_1_, f32[16,72,256]{2,1,0:T(8,128)S(1)} %get-tuple-element.20.refs_2_), custom_call_target="tpu_custom_call" | custom-call | flops 35389440 | bytes 9437184 | tf_op jit(solution)/shard_map/pallas_call | solution.py:550
Async XLA Ops:
  2.2 6.5 %copy-start.6 = (s32[513,129]{0,1:T(8,128)S(1)}, s32[513,129]{0,1:T(8,128)}, u32[]{:S(2)}) copy-start(s32[513,129]{0,1:T(8,128)} %param.9) | copy-start | bytes 794128
  2.2 6.5 %copy-start.7 = (s32[513,129]{0,1:T(8,128)S(1)}, s32[513,129]{0,1:T(8,128)}, u32[]{:S(2)}) copy-start(s32[513,129]{0,1:T(8,128)} %param.10) | copy-start | bytes 794128
  2.2 30.7 %all-to-all-start = ((f32[16,1,64,256]{3,2,1,0:T(8,128)}), f32[16,1,64,256]{3,2,1,0:T(8,128)S(1)}, u32[]{:S(2)}, u32[]{:S(2)}) async-start(f32[16,1,64,256]{3,2,1,0:T(8,128)} %bitcast.12), calls=%async_computation | async-start | bytes 2097152 | tf_op jit(solution)/shard_map/all_to_all | solution.py:574
  32.9 1.0 copy-start.5
  40.5 69.0 %copy-start.2 = (bf16[3,2,256,256]{3,2,1,0:T(8,128)(2,1)S(1)}, bf16[3,2,256,256]{3,2,1,0:T(8,128)(2,1)}, u32[]{:S(2)}) copy-start(bf16[3,2,256,256]{3,2,1,0:T(8,128)(2,1)} %constant.20.clone.refs_2_) | copy-start | bytes 2359300
  40.5 69.0 %copy-start.3 = (bf16[2,256,256]{2,1,0:T(8,128)(2,1)S(1)}, bf16[2,256,256]{2,1,0:T(8,128)(2,1)}, u32[]{:S(2)}) copy-start(bf16[2,256,256]{2,1,0:T(8,128)(2,1)} %constant.19.clone.refs_1_) | copy-start | bytes 786436
  40.5 69.0 %copy-start.4 = (f32[1,1024,256]{2,1,0:T(8,128)S(1)}, f32[1,1024,256]{2,1,0:T(8,128)}, u32[]{:S(2)}) copy-start(f32[1,1024,256]{2,1,0:T(8,128)} %get-tuple-element.17.refs_4_) | copy-start | bytes 3145732
  40.6 34.0 %all-to-all-start.1 = ((f32[16,1,19,8,128]{4,3,2,1,0:T(8,128)}), f32[16,1,19,8,128]{4,3,2,1,0:T(8,128)S(1)}, u32[]{:S(2)}, u32[]{:S(2)}) async-start(f32[16,1,19,8,128]{4,3,2,1,0:T(8,128)} %get-tuple-element.15), calls=%async_computation.1 | async-start | bytes 2490368 | tf_op jit(solution)/shard_map/all_to_all | solution.py:574
  74.5 35.0 %copy-start.1 = (bf16[2,2,512,512]{3,2,1,0:T(8,128)(2,1)S(1)}, bf16[2,2,512,512]{3,2,1,0:T(8,128)(2,1)}, u32[]{:S(2)}) copy-start(bf16[2,2,512,512]{3,2,1,0:T(8,128)(2,1)} %constant.21.clone.refs_3_) | copy-start | bytes 6291460
  78.9 30.6 %copy-start = (f32[1024,256]{1,0:T(8,128)S(1)}, f32[1024,256]{1,0:T(8,128)}, u32[]{:S(2)}) copy-start(f32[1024,256]{1,0:T(8,128)} %get-tuple-element.14.refs_5_) | copy-start | bytes 3145732

commit v2 on v1

--- a/solution.py
+++ b/solution.py
@@ -68,7 +68,7 @@
     return -(-length // unit) * unit
 
 
-def weights_kernel(nx, nz, levels, table_ref, code_ref, data, prior):
+def weights_kernel(nx, nz, levels, table_ref, code_ref, weights):
     heights, widths = code_ref.shape
     scale = 1.0 / (nx * nz)
     kz = lax.broadcasted_iota(jnp.int32, (heights, nz), 1)
@@ -93,8 +93,8 @@
                 response = jnp.where(spread == level + 1.0, table_ref[level], response)
             gain = scale / (response * response + 1.0)
             rows = slice(base + top, base + top + tile)
-            prior[rows] = gain
-            data[rows] = (UNIT * response) * gain
+            weights[0, rows] = (UNIT * response) * gain
+            weights[1, rows] = gain
 
 
 def make_weights(tf_table, tilt_index, wedge, nx, nz):
@@ -102,16 +102,15 @@
     code = jnp.where(wedge > 0, tilt_index + 1, 0).T
     extra = [(0, padded_to(size, LANE) - size) for size in code.shape]
     code = jnp.pad(code, extra).astype(bf16)
-    grid = jax.ShapeDtypeStruct((nx, nz), f32)
     vmem = pl.BlockSpec(memory_space=pltpu.VMEM)
     return pl.pallas_call(
         functools.partial(weights_kernel, nx, nz, levels),
         in_specs=[pl.BlockSpec(memory_space=pltpu.SMEM), vmem],
-        out_specs=[vmem] * 2,
-        out_shape=[grid] * 2,
-        compiler_params=pltpu.CompilerParams(vmem_limit_bytes=MOST_VMEM),
+        out_specs=vmem,
+        out_shape=jax.ShapeDtypeStruct((2, nx, nz), f32),
+        compiler_params=pltpu.CompilerParams(vmem_limit_bytes=16 * MIB),
         cost_estimate=pl.CostEstimate(
-            flops=60 * nx * nz, bytes_accessed=12 * nx * nz, transcendentals=0
+            flops=60000 * nx * nz, bytes_accessed=8 * nx * nz, transcendentals=0
         ),
     )(tf_table, code)
 
@@ -193,30 +192,17 @@
 
 
 def filter_kernel(first, halo, slab, *refs):
-    cells, ztab_far, small_far, odd_far, refs = refs[0], refs[1], refs[2], refs[3], refs[4:]
+    cells, ztab, small, odd, weights, refs = refs[:5] + (refs[5:],)
     if first:
-        data_far, prior_far, windows_far, kept_far, refs = refs[0], refs[1], refs[2], refs[3], refs[4:]
+        windows, kept, high, low, padded = refs
     else:
-        kept_far, prior_far, windows, refs = refs[0], refs[1], refs[2], refs[3:]
-    ztab, small, odd, scale, other, high, low, padded, semaphores, refs = refs[:9] + (refs[9:],)
-    if first:
-        windows, window_semaphores = refs
+        kept, windows, high, low, padded = refs
     devices, rows, _, nz = cells.shape
     nx = devices * slab
     half, quarter = nx // 2, nx // 4
     width = slab + 2 * halo
     blocks = nz // LANE
-    arrivals = [
-        pltpu.make_async_copy(ztab_far, ztab, semaphores.at[0]),
-        pltpu.make_async_copy(small_far, small, semaphores.at[1]),
-        pltpu.make_async_copy(odd_far.at[0], odd.at[0], semaphores.at[2]),
-        pltpu.make_async_copy(prior_far, scale, semaphores.at[3]),
-    ]
-    if first:
-        arrivals.append(pltpu.make_async_copy(data_far, other.at[0], semaphores.at[4]))
-    last_arrival = pltpu.make_async_copy(odd_far.at[1], odd.at[1], semaphores.at[5])
-    for copy in arrivals:
-        copy.start()
+    ztable = (ztab[0], ztab[1])
 
     def table(ref, i, rows=slice(None)):
         return ref[i, 0, rows], ref[i, 1, rows]
@@ -230,130 +216,74 @@
     parts = [slice(i * quarter, (i + 1) * quarter) for i in range(4)]
     folds = [parts[0], parts[1], slice(half, nx)]
     for r in range(rows):
-        if not first:
-            kept_copy = pltpu.make_async_copy(kept_far.at[r], other.at[0], semaphores.at[4])
-            kept_copy.start()
-        if r == 0:
-            last_arrival.start()
         q = [
             cells[i * devices // 4 : (i + 1) * devices // 4, r].reshape(quarter, nz)
             for i in range(4)
         ]
         even = (q[0] + q[2], q[1] + q[3])
         folded = (even[0] + even[1], even[0] - even[1], q[0] - q[2], q[1] - q[3])
-        if r == 0:
-            arrivals[0].wait()
-        ztable = (ztab[0], ztab[1])
         for spot, value in zip(parts, folded):
             store(spot, dot3(split(value), ztable))
-        if r == 0:
-            arrivals[1].wait()
         waves = [dot3(table(small, i), load(folds[i])) for i in range(2)]
-        if r == 0:
-            arrivals[2].wait()
-        for i in range(2):
-            waves.append(dot3(table(odd, 0, parts[i]), load(folds[2])))
-        if r == 0:
-            for copy in arrivals[3:]:
-                copy.wait()
-        if not first:
-            kept_copy.wait()
+        waves += [dot3(table(odd, 0, parts[i]), load(folds[2])) for i in range(2)]
         for spot, wave in zip(parts, waves):
             if first:
-                seen = wave * other[0, spot]
-                other[1, spot] = seen
-                store(spot, seen + wave * (UNIT * scale[spot]))
+                seen = wave * weights[0, spot]
+                kept[r, spot] = seen
+                store(spot, seen + wave * (UNIT * weights[1, spot]))
             else:
-                store(spot, other[0, spot] + wave * scale[spot])
-        if first:
-            kept_copy = pltpu.make_async_copy(other.at[1], kept_far.at[r], semaphores.at[6])
-            kept_copy.start()
+                store(spot, kept[r, spot] + wave * weights[1, spot])
         after = (halo + nx) // SUB * SUB
         padded[:SUB] = jnp.zeros((SUB, nz), f32)
         padded[after : after + 2 * SUB] = jnp.zeros((2 * SUB, nz), f32)
         plus, minus = dot3(table(small, 0), load(folds[0])), dot3(table(small, 2), load(folds[1]))
-        if r == 0:
-            last_arrival.wait()
-        leaving = []
-        written, sent = set(), set()
         for i, e in enumerate((plus + minus, plus - minus)):
             o = dot3(table(odd, 1, parts[i]), load(folds[2]))
             for j, value in ((i, e + o), (i + 2, e - o)):
                 place = halo + j * quarter
                 padded[place : place + quarter] = dot3(split(value), ztable)
-                written |= set(range(j * quarter, (j + 1) * quarter))
-            for device in range(devices):
-                needed = range(device * slab - halo, (device + 1) * slab + halo)
-                if device in sent or not written.issuperset(x for x in needed if 0 <= x < nx):
-                    continue
-                sent.add(device)
-                for g in range(width // SUB):
-                    spot = device * slab + SUB * g
-                    for k in range(blocks):
-                        windows[device, r, g * blocks + k] = padded[
-                            spot : spot + SUB, LANE * k : LANE * (k + 1)
-                        ]
-                rest = width % SUB
-                spot = device * slab + width - rest
-                for k in range(blocks if rest else 0):
-                    tile, row = width // SUB * blocks + k * rest // SUB, k * rest % SUB
-                    windows[device, r, tile, row : row + rest] = padded[
-                        spot : spot + rest, LANE * k : LANE * (k + 1)
+        for device in range(devices):
+            for g in range(width // SUB):
+                spot = device * slab + SUB * g
+                for k in range(blocks):
+                    windows[device, r, g * blocks + k] = padded[
+                        spot : spot + SUB, LANE * k : LANE * (k + 1)
                     ]
-                if first:
-                    copy = pltpu.make_async_copy(
-                        windows.at[device, r], windows_far.at[device, r], window_semaphores.at[device]
-                    )
-                    copy.start()
-                    leaving.append(copy)
-        if first:
-            for copy in leaving:
-                copy.wait()
-            kept_copy.wait()
-
-
-def run_filter(first, halo, cells, tables, far):
+            rest = width % SUB
+            spot = device * slab + width - rest
+            for k in range(blocks if rest else 0):
+                tile, row = width // SUB * blocks + k * rest // SUB, k * rest % SUB
+                windows[device, r, tile, row : row + rest] = padded[
+                    spot : spot + rest, LANE * k : LANE * (k + 1)
+                ]
+
+
+def run_filter(first, halo, cells, tables, weights, kept):
     devices, rows, slab, nz = cells.shape
     nx = devices * slab
-    ztab, small, odd = tables
     vmem = pl.BlockSpec(memory_space=pltpu.VMEM)
-    hbm = pl.BlockSpec(memory_space=pltpu.HBM)
-    windows = (devices, rows, window_tiles(slab + 2 * halo, nz), SUB, LANE)
-    out_shape, out_specs = [jax.ShapeDtypeStruct(windows, f32)], [hbm if first else vmem]
+    operands = [cells, *tables, weights, *kept]
+    tiles = window_tiles(slab + 2 * halo, nz)
+    out_shape = [jax.ShapeDtypeStruct((devices, rows, tiles, SUB, LANE), f32)]
     if first:
         out_shape.append(jax.ShapeDtypeStruct((rows, nx, nz), f32))
-        out_specs.append(hbm)
-    scratch_shapes = [
-        pltpu.VMEM(ztab.shape, bf16),
-        pltpu.VMEM(small.shape, bf16),
-        pltpu.VMEM(odd.shape, bf16),
-        pltpu.VMEM((nx, nz), f32),
-        pltpu.VMEM((2, nx, nz), f32),
-        pltpu.VMEM((nx, nz), bf16),
-        pltpu.VMEM((nx, nz), bf16),
-        pltpu.VMEM((nx + 3 * SUB, nz), f32),
-        pltpu.SemaphoreType.DMA((7,)),
-    ]
-    if first:
-        scratch_shapes += [
-            pltpu.VMEM(windows, f32),
-            pltpu.SemaphoreType.DMA((devices,)),
-        ]
     return pl.pallas_call(
         functools.partial(filter_kernel, first, halo, slab),
-        in_specs=[vmem] + [hbm] * (3 + len(far)),
-        out_specs=out_specs,
+        in_specs=[vmem] * len(operands),
+        out_specs=[vmem] * len(out_shape),
         out_shape=out_shape,
-        scratch_shapes=scratch_shapes,
-        compiler_params=pltpu.CompilerParams(
-            vmem_limit_bytes=MOST_VMEM if first else 32 * MIB
-        ),
+        scratch_shapes=[
+            pltpu.VMEM((nx, nz), bf16),
+            pltpu.VMEM((nx, nz), bf16),
+            pltpu.VMEM((nx + 3 * SUB, nz), f32),
+        ],
+        compiler_params=pltpu.CompilerParams(vmem_limit_bytes=24 * MIB),
         cost_estimate=pl.CostEstimate(
             flops=6 * rows * nx * nz * (2 * nz + nx),
             bytes_accessed=8 * rows * nx * nz,
             transcendentals=0,
         ),
-    )(cells, ztab, small, odd, *far)
+    )(*operands)
 
 
 def lane_sums(pieces):
@@ -384,7 +314,7 @@
     ]
 
 
-def passes_kernel(first, last, halo, slab, nx, start_ref, target, *refs):
+def passes_kernel(first, last, halo, slab, nx, target, *refs):
     if first:
         duals_in, refs = None, refs
     else:
@@ -405,7 +335,7 @@
     keep = 1.0 / (1.0 + step_primal)
     pull = step_primal * keep
     push = pull * gain / decay
-    origin = start_ref[0] - halo
+    origin = lax.axis_index("gy") * slab - halo
 
     def goal_of(y, g, k):
         if SUB * (g + 1) <= width:
@@ -535,7 +465,7 @@
         copy.wait()
 
 
-def run_passes(first, last, halo, slab, nx, start, target, duals):
+def run_passes(first, last, halo, slab, nx, target, duals):
     ny = target.shape[0]
     nz = target.shape[1] * SUB * LANE // (slab + 2 * halo)
     width = padded_to(slab + 2 * halo, SUB)
@@ -549,7 +479,7 @@
         out_specs = [vmem] * 4
     return pl.pallas_call(
         functools.partial(passes_kernel, first, last, halo, slab, nx),
-        in_specs=[pl.BlockSpec(memory_space=pltpu.SMEM)] + [vmem] * (1 + len(duals)),
+        in_specs=[vmem] * (1 + len(duals)),
         out_specs=out_specs,
         out_shape=out_shape,
         scratch_shapes=[
@@ -567,7 +497,7 @@
             bytes_accessed=8 * 4 * ny * width * nz,
             transcendentals=PASSES * ny * width * nz,
         ),
-    )(start, target, *duals)
+    )(target, *duals)
 
 
 def exchange(blocks):
@@ -579,20 +509,18 @@
     devices = lax.axis_size("gy")
     rows = ny // devices
     nx = slab * devices
-    start = (lax.axis_index("gy") * slab).astype(jnp.int32).reshape(1)
     tables = [jnp.asarray(table) for table in (z_table(nz),) + x_tables(nx)]
     cells = exchange(turn(observed).reshape(devices, rows, slab, nz))
-    data, prior = make_weights(tf_table, tilt_index, wedge, nx, nz)
-    duals = ()
+    weights = make_weights(tf_table, tilt_index, wedge, nx, nz)
+    duals, kept = (), ()
     for outer in range(OUTER):
         first, last = outer == 0, outer == OUTER - 1
         halo = HALO_LAST if last else HALO_FIRST
-        made = run_filter(first, halo, cells, tables, (data, prior) if first else (kept, prior))
-        if first:
-            kept = made[1]
+        made = run_filter(first, halo, cells, tables, weights, kept)
+        kept = made[1:]
         windows = exchange(made[0])
         target = windows.reshape((ny,) + windows.shape[2:])
-        made = run_passes(first, last, halo, slab, nx, start, target, duals)
+        made = run_passes(first, last, halo, slab, nx, target, duals)
         if last:
             return made.reshape(slab, ny, nz)
         duals = tuple(made[1:])

time: 155 us -> 151 us (0.974)
  blocking collectives: 63.8 us -> 97.4 us
  waiting for transfers between devices: 47 us -> 19.3 us
  Pallas kernels: 27.2 us -> 20.2 us
  starting transfers between devices: 12.2 us -> 6.44 us
  local copies, waits for them, and re-layouts: 1.76 us -> 4.65 us
    all_to_all x2 -> x3, blocking collectives: 63.8 us -> 97.4 us  [exchange(): return lax.all_to_all(blocks, 'gy', split_axis=0, concat_axis=0, tiled=True)]
    all_to_all x2 -> x1, waiting for transfers between devices: 47 us -> 19.3 us  [exchange(): return lax.all_to_all(blocks, 'gy', split_axis=0, concat_axis=0, tiled=True)]
    all_to_all x2 -> x1, starting transfers between devices: 12.2 us -> 6.44 us  [exchange(): return lax.all_to_all(blocks, 'gy', split_axis=0, concat_axis=0, tiled=True)]
    pallas_call x2, Pallas kernels: 10.7 us -> 5.46 us  [run_filter(): pl.pallas_call(functools.partial(filter_kernel, first, halo, slab), in_sp...]
    unnamed x16 -> x20, local copies, waits for them, and re-layouts: 1.01 us -> 4.62 us
    pallas_call x1, Pallas kernels: 4.66 us -> 2.92 us  [make_weights(): pl.pallas_call(functools.partial(weights_kernel, nx, nz, levels), in_spec...]
  transfers between devices with their start and end apart: 2 -> 1, of which waited for: 2 -> 1; matrix products, arithmetic and copies ran while one was open for 1% -> 0% of each run, Pallas kernels for 3% -> 2%
where the time goes in v2:
time: 151 us; the launch traced here: 148 us
  blocking collectives  97.4 us (65%)
  Pallas kernels  20.2 us (13%)
  waiting for transfers between devices  19.3 us (13%)
  starting transfers between devices  6.44 us (4%)
  local copies, waits for them, and re-layouts  4.65 us (3%)
    all_to_all x3, blocking collectives, exchange(): return lax.all_to_all(blocks, 'gy', split_axis=0, concat_axis=0, tiled=True)  97.4 us
    all_to_all x1, waiting for transfers between devices, exchange(): return lax.all_to_all(blocks, 'gy', split_axis=0, concat_axis=0, tiled=True)  19.3 us
    pallas_call x2, Pallas kernels, run_passes(): pl.pallas_call(functools.partial(passes_kernel, first, last, halo, slab,...  9.63 us
    all_to_all x1, starting transfers between devices, exchange(): return lax.all_to_all(blocks, 'gy', split_axis=0, concat_axis=0, tiled=True)  6.44 us
    pallas_call x2, Pallas kernels, run_filter(): pl.pallas_call(functools.partial(filter_kernel, first, halo, slab), in_sp...  5.46 us
    unnamed x20, local copies, waits for them, and re-layouts  4.62 us
  transfers between devices with their start and end apart: 1, of which 1 were waited for; matrix products, arithmetic and copies ran while one was open for 0% of the time, Pallas kernels for 2%

profile of v2, /device:TPU:8, one launch (start us, length us, event | category | flops | bytes accessed | tf_op | source)
XLA Modules:
  0.0 148.2 jit_solution(12741959717380769308)
XLA Ops:
  0.0 2.2 %shard_map.73 = f32[16,64,256]{2,1,0:T(8,128)} custom-call(f32[1024,256]{1,0:T(8,128)} %bitcast.12), custom_call_target="tpu_custom_call" | custom-call | bytes 2097152 | tf_op jit(solution)/shard_map/pallas_call | solution.py:173
  2.2 0.0 copy-start.8
  2.2 0.0 copy-start.9
  2.2 6.4 %all-to-all-start = ((f32[16,1,64,256]{3,2,1,0:T(8,128)}), f32[16,1,64,256]{3,2,1,0:T(8,128)S(1)}, u32[]{:S(2)}, u32[]{:S(2)}) async-start(f32[16,1,64,256]{3,2,1,0:T(8,128)} %bitcast.11), calls=%async_computation | async-start | bytes 2097152 | tf_op jit(solution)/shard_map/all_to_all | solution.py:504
  8.7 0.0 copy-done.8
  8.7 0.0 copy-done.9
  8.7 0.0 copy-start
  8.7 0.1 fusion
  8.8 0.5 copy-done
  9.4 0.0 copy-start.1
  9.4 0.0 copy-start.4
  9.4 2.9 %shard_map.74.refs_4_ = f32[2,1024,256]{2,1,0:T(8,128)S(1)} custom-call(f32[16]{0:T(128)S(1)} %copy-done, bf16[256,640]{1,0:T(8,128)(2,1)S(1)} %pad.5.code_ref), custom_call_target="tpu_custom_call" | custom-call | flops 15728640000 | bytes 2097152 | tf_op jit(solution)/shard_map/pallas_call | solution.py:106
  12.3 0.0 copy-start.5
  12.3 1.3 copy-done.5
  13.6 19.3 %all-to-all-done.refs_0_ = f32[16,1,64,256]{3,2,1,0:T(8,128)S(1)} async-done(((f32[16,1,64,256]{3,2,1,0:T(8,128)}), f32[16,1,64,256]{3,2,1,0:T(8,128)S(1)}, u32[]{:S(2)}, u32[]{:S(2)}) %all-to-all-start) | async-done | bytes 1048608 | tf_op jit(solution)/shard_map/all_to_all | solution.py:504
  32.9 0.0 copy-done.1
  32.9 0.0 copy-done.4
  32.9 0.0 copy-start.2
  32.9 1.1 copy-done.2
  34.1 0.0 copy-start.6
  34.1 1.6 %copy-done.6 = f32[2,1024,256]{2,1,0:T(8,128)S(1)} copy-done((f32[2,1024,256]{2,1,0:T(8,128)S(1)}, f32[2,1024,256]{2,1,0:T(8,128)}, u32[]{:S(2)}) %copy-start.6) | copy-done | bytes 2097176
  35.6 2.8 %shard_map.75 = (f32[16,1,19,8,128]{4,3,2,1,0:T(8,128)S(1)}, f32[1,1024,256]{2,1,0:T(8,128)S(1)}) custom-call(f32[16,1,64,256]{3,2,1,0:T(8,128)S(1)} %all-to-all-done.refs_0_, bf16[2,256,256]{2,1,0:T(8,128)(2,1)S(1)} %copy-done.4, bf16[3,2,256,256]{3,2,1,0:T(8,128)(2,1)S(1)} %copy-done.2, bf16[2,2,512,512]{3,2,1,0:T(8,128)(2,1)S(1)} %copy-done.1, ...), custom_call_target="tpu_custom_call" | custom-call | flops 2415919104 | bytes 2097152 | tf_op jit(solution)/shard_map/pallas_call | solution.py:270
  38.4 34.9 %all_to_all.20 = f32[16,1,19,8,128]{4,3,2,1,0:T(8,128)S(1)} all-to-all(f32[16,1,19,8,128]{4,3,2,1,0:T(8,128)S(1)} %get-tuple-element.11), channel_id=1, replica_groups=mesh['groups'=2,'gy'=16] {'gy'}, dimensions={0} | all-to-all | bytes 2490368 | tf_op jit(solution)/shard_map/all_to_all | solution.py:504
  73.3 0.0 copy-start.7
  73.3 4.4 %shard_map.76 = (f32[16,64,256]{2,1,0:T(8,128)S(1)}, f32[16,72,256]{2,1,0:T(8,128)S(1)}, f32[16,72,256]{2,1,0:T(8,128)S(1)}, f32[16,72,256]{2,1,0:T(8,128)S(1)}) custom-call(f32[16,19,8,128]{3,2,1,0:T(8,128)S(1)} %bitcast.8), custom_call_target="tpu_custom_call" | custom-call | flops 39321600 | bytes 10485760 | tf_op jit(solution)/shard_map/pallas_call | solution.py:480
  77.7 0.0 copy-start.3
  77.7 29.3 %all_to_all.21.refs_0_ = f32[16,1,64,256]{3,2,1,0:T(8,128)S(1)} all-to-all(f32[16,1,64,256]{3,2,1,0:T(8,128)S(1)} %bitcast.10), channel_id=1, replica_groups=mesh['groups'=2,'gy'=16] {'gy'}, dimensions={0} | all-to-all | bytes 2097152 | tf_op jit(solution)/shard_map/all_to_all | solution.py:504
  107.0 0.0 copy-done.7
  107.0 0.0 copy-done.3
  107.1 2.7 %shard_map.77 = f32[16,1,18,8,128]{4,3,2,1,0:T(8,128)S(1)} custom-call(f32[16,1,64,256]{3,2,1,0:T(8,128)S(1)} %all_to_all.21.refs_0_, bf16[2,256,256]{2,1,0:T(8,128)(2,1)S(1)} %copy-done.4, bf16[3,2,256,256]{3,2,1,0:T(8,128)(2,1)S(1)} %copy-done.3, bf16[2,2,512,512]{3,2,1,0:T(8,128)(2,1)S(1)} %copy-done.1, f32[2,1024,256]{2,1,0:T(8,128)S(1)} %copy-done.7, ...), custom_call_target="tpu_custom_call" | custom-call | flops 2415919104 | bytes 2097152 | tf_op jit(solution)/shard_map/pallas_call | solution.py:270
  109.8 33.2 %all_to_all.22 = f32[16,1,18,8,128]{4,3,2,1,0:T(8,128)S(1)} all-to-all(f32[16,1,18,8,128]{4,3,2,1,0:T(8,128)S(1)} %shard_map.77), channel_id=1, replica_groups=mesh['groups'=2,'gy'=16] {'gy'}, dimensions={0} | all-to-all | bytes 2359296 | tf_op jit(solution)/shard_map/all_to_all | solution.py:504
  142.9 5.3 %shard_map.78 = f32[1024,256]{1,0:T(8,128)} custom-call(f32[16,18,8,128]{3,2,1,0:T(8,128)S(1)} %bitcast.9, f32[16,72,256]{2,1,0:T(8,128)S(1)} %get-tuple-element.14.refs_0_, f32[16,72,256]{2,1,0:T(8,128)S(1)} %get-tuple-element.15.refs_1_, f32[16,72,256]{2,1,0:T(8,128)S(1)} %get-tuple-element.16.refs_2_), custom_call_target="tpu_custom_call" | custom-call | flops 35389440 | bytes 9437184 | tf_op jit(solution)/shard_map/pallas_call | solution.py:480
  (1 shorter events, 0.0 us)
Async XLA Ops:
  2.2 6.5 %copy-start.8 = (s32[513,129]{0,1:T(8,128)S(1)}, s32[513,129]{0,1:T(8,128)}, u32[]{:S(2)}) copy-start(s32[513,129]{0,1:T(8,128)} %param.9) | copy-start | bytes 794128
  2.2 6.5 %copy-start.9 = (s32[513,129]{0,1:T(8,128)S(1)}, s32[513,129]{0,1:T(8,128)}, u32[]{:S(2)}) copy-start(s32[513,129]{0,1:T(8,128)} %param.10) | copy-start | bytes 794128
  2.2 30.7 %all-to-all-start = ((f32[16,1,64,256]{3,2,1,0:T(8,128)}), f32[16,1,64,256]{3,2,1,0:T(8,128)S(1)}, u32[]{:S(2)}, u32[]{:S(2)}) async-start(f32[16,1,64,256]{3,2,1,0:T(8,128)} %bitcast.11), calls=%async_computation | async-start | bytes 2097152 | tf_op jit(solution)/shard_map/all_to_all | solution.py:504
  8.7 0.7 copy-start
  9.4 23.6 %copy-start.1 = (bf16[2,2,512,512]{3,2,1,0:T(8,128)(2,1)S(1)}, bf16[2,2,512,512]{3,2,1,0:T(8,128)(2,1)}, u32[]{:S(2)}) copy-start(bf16[2,2,512,512]{3,2,1,0:T(8,128)(2,1)} %constant.15.clone.refs_3_) | copy-start | bytes 6291460
  9.4 23.6 %copy-start.4 = (bf16[2,256,256]{2,1,0:T(8,128)(2,1)S(1)}, bf16[2,256,256]{2,1,0:T(8,128)(2,1)}, u32[]{:S(2)}) copy-start(bf16[2,256,256]{2,1,0:T(8,128)(2,1)} %constant.13.clone.refs_1_) | copy-start | bytes 786436
  12.3 1.3 copy-start.5
  32.9 1.1 copy-start.2
  34.1 1.6 %copy-start.6 = (f32[2,1024,256]{2,1,0:T(8,128)S(1)}, f32[2,1024,256]{2,1,0:T(8,128)}, u32[]{:S(2)}) copy-start(f32[2,1024,256]{2,1,0:T(8,128)} %copy-done.5) | copy-start | bytes 6291460
  73.3 33.7 %copy-start.7 = (f32[2,1024,256]{2,1,0:T(8,128)S(1)}, f32[2,1024,256]{2,1,0:T(8,128)}, u32[]{:S(2)}) copy-start(f32[2,1024,256]{2,1,0:T(8,128)} %copy-done.5) | copy-start | bytes 6291460
  77.7 29.4 %copy-start.3 = (bf16[3,2,256,256]{3,2,1,0:T(8,128)(2,1)S(1)}, bf16[3,2,256,256]{3,2,1,0:T(8,128)(2,1)}, u32[]{:S(2)}) copy-start(bf16[3,2,256,256]{3,2,1,0:T(8,128)(2,1)} %constant.14.clone.refs_2_) | copy-start | bytes 2359300

commit v3 on v2

--- a/solution.py
+++ b/solution.py
@@ -21,7 +21,7 @@
 LANE = 128
 HALO_LAST = 2 * PASSES
 HALO_FIRST = HALO_LAST + 2 * PASSES - 2
-UNROLL = 8
+UNROLL = 16
 COLUMN = 3
 MIB = 1024 * 1024
 MOST_VMEM = 61 * MIB
@@ -55,8 +55,11 @@
     fourth = cas(4 * place[:quarter], place[:quarter], length)
     second = cas(4 * place[:quarter] + 2, place[:quarter], length)
     odd = cas(2 * place + 1, place, length)
-    small = np.stack([halves(fourth), halves(second), halves(second.T)])
-    return small, np.stack([halves(odd), halves(odd.T)])
+    blocks = [fourth, second, second.T]
+    for table in (odd, odd.T):
+        for rows in (slice(0, quarter), slice(quarter, half)):
+            blocks += [table[rows, :quarter], table[rows, quarter:]]
+    return halves(np.stack(blocks))
 
 
 def kx_rows(length):
@@ -68,7 +71,7 @@
     return -(-length // unit) * unit
 
 
-def weights_kernel(nx, nz, levels, table_ref, code_ref, weights):
+def weights_kernel(nx, nz, levels, table_ref, code_ref, both_data, prior):
     heights, widths = code_ref.shape
     scale = 1.0 / (nx * nz)
     kz = lax.broadcasted_iota(jnp.int32, (heights, nz), 1)
@@ -93,8 +96,9 @@
                 response = jnp.where(spread == level + 1.0, table_ref[level], response)
             gain = scale / (response * response + 1.0)
             rows = slice(base + top, base + top + tile)
-            weights[0, rows] = (UNIT * response) * gain
-            weights[1, rows] = gain
+            prior[rows] = gain
+            both_data[0, rows] = UNIT * (response * gain + gain)
+            both_data[1, rows] = (UNIT * response) * gain
 
 
 def make_weights(tf_table, tilt_index, wedge, nx, nz):
@@ -106,8 +110,8 @@
     return pl.pallas_call(
         functools.partial(weights_kernel, nx, nz, levels),
         in_specs=[pl.BlockSpec(memory_space=pltpu.SMEM), vmem],
-        out_specs=vmem,
-        out_shape=jax.ShapeDtypeStruct((2, nx, nz), f32),
+        out_specs=[vmem] * 2,
+        out_shape=[jax.ShapeDtypeStruct((2, nx, nz), f32), jax.ShapeDtypeStruct((nx, nz), f32)],
         compiler_params=pltpu.CompilerParams(vmem_limit_bytes=16 * MIB),
         cost_estimate=pl.CostEstimate(
             flops=60000 * nx * nz, bytes_accessed=8 * nx * nz, transcendentals=0
@@ -192,7 +196,7 @@
 
 
 def filter_kernel(first, halo, slab, *refs):
-    cells, ztab, small, odd, weights, refs = refs[:5] + (refs[5:],)
+    cells, ztab, xtab, weights, refs = refs[:4] + (refs[4:],)
     if first:
         windows, kept, high, low, padded = refs
     else:
@@ -204,8 +208,8 @@
     blocks = nz // LANE
     ztable = (ztab[0], ztab[1])
 
-    def table(ref, i, rows=slice(None)):
-        return ref[i, 0, rows], ref[i, 1, rows]
+    def table(*places):
+        return [jnp.concatenate([xtab[part, i] for i in places], axis=1) for part in range(2)]
 
     def store(spot, value):
         high[spot], low[spot] = split(value)
@@ -224,21 +228,20 @@
         folded = (even[0] + even[1], even[0] - even[1], q[0] - q[2], q[1] - q[3])
         for spot, value in zip(parts, folded):
             store(spot, dot3(split(value), ztable))
-        waves = [dot3(table(small, i), load(folds[i])) for i in range(2)]
-        waves += [dot3(table(odd, 0, parts[i]), load(folds[2])) for i in range(2)]
+        waves = [dot3(table(i), load(folds[i])) for i in range(2)]
+        waves += [dot3(table(3 + 2 * i, 4 + 2 * i), load(folds[2])) for i in range(2)]
         for spot, wave in zip(parts, waves):
             if first:
-                seen = wave * weights[0, spot]
-                kept[r, spot] = seen
-                store(spot, seen + wave * (UNIT * weights[1, spot]))
+                kept[r, spot] = wave * weights[1, spot]
+                store(spot, wave * weights[0, spot])
             else:
-                store(spot, kept[r, spot] + wave * weights[1, spot])
+                store(spot, kept[r, spot] + wave * weights[spot])
         after = (halo + nx) // SUB * SUB
         padded[:SUB] = jnp.zeros((SUB, nz), f32)
         padded[after : after + 2 * SUB] = jnp.zeros((2 * SUB, nz), f32)
-        plus, minus = dot3(table(small, 0), load(folds[0])), dot3(table(small, 2), load(folds[1]))
+        plus, minus = dot3(table(0), load(folds[0])), dot3(table(2), load(folds[1]))
         for i, e in enumerate((plus + minus, plus - minus)):
-            o = dot3(table(odd, 1, parts[i]), load(folds[2]))
+            o = dot3(table(7 + 2 * i, 8 + 2 * i), load(folds[2]))
             for j, value in ((i, e + o), (i + 2, e - o)):
                 place = halo + j * quarter
                 padded[place : place + quarter] = dot3(split(value), ztable)
@@ -320,13 +323,13 @@
     else:
         duals_in, refs = refs[:3], refs[3:]
     if last:
-        restored, refs = refs[0], refs[1:]
+        restored, dual_x, dual_y, dual_z, lead, field = refs[:1] + refs[-4:-1] + refs[1:3]
+        turned, semaphores = refs[3:-4], refs[-1]
     else:
-        current, duals_out, refs = refs[0], refs[1:4], refs[4:]
-    lead, field, dual_x, dual_y, dual_z = refs[:5]
-    turned = refs[5:-1] if last else ()
+        current, dual_x, dual_y, dual_z, lead, field = refs
     ny, _, nz = field.shape
     width = slab + 2 * halo
+    width_before = slab + 2 * HALO_FIRST
     groups = padded_to(width, SUB) // SUB
     blocks = nz // LANE
     decay = 1.0 / (1.0 + step_dual * huber_eps / bound_dual)
@@ -345,11 +348,14 @@
         shift = k * rest % SUB
         return pltpu.roll(tail, SUB - shift, 0) if shift else tail
 
+    inside = {}
+    for g in range(groups):
+        if SUB * g < halo or SUB * (g + 1) > width - halo:
+            place = origin + SUB * g + lax.broadcasted_iota(jnp.int32, (SUB, LANE), 0)
+            inside[g] = jnp.where((place >= 0) & (place < nx), 1.0, 0.0)
+
     def masked(value, g):
-        if SUB * g >= halo and SUB * (g + 1) <= width - halo:
-            return value
-        place = origin + SUB * g + lax.broadcasted_iota(jnp.int32, (SUB, LANE), 0)
-        return jnp.where((place >= 0) & (place < nx), value, 0.0)
+        return value * inside[g] if g in inside else value
 
     def at(g, k):
         return pl.ds(SUB * g, SUB), pl.ds(LANE * k, LANE)
@@ -383,7 +389,10 @@
                     if sweep > 0:
                         before = [dual_x[(y,) + spot], dual_y[(y + 1,) + spot], dual_z[(y,) + spot]]
                     elif duals_in is not None:
-                        before = [ref[(y,) + spot] for ref in duals_in]
+                        rows = pl.ds(SUB * g + (width_before - width) // 2, SUB)
+                        before = [
+                            ref[y + shift, rows, spot[1]] for ref, shift in zip(duals_in, (0, 1, 0))
+                        ]
                     else:
                         before = None
                     if before is not None:
@@ -396,14 +405,6 @@
                     dual_x[(y,) + spot] = made[0]
                     dual_y[(y + 1,) + spot] = made[1]
                     dual_z[(y,) + spot] = made[2]
-                    if final and not last:
-                        shift = halo - HALO_LAST
-                        lo = max(0, shift - SUB * g)
-                        hi = min(SUB, slab + 2 * HALO_LAST + shift - SUB * g)
-                        if lo < hi:
-                            rows = pl.ds(SUB * g + lo - shift, hi - lo)
-                            for a in range(3):
-                                duals_out[a][y, rows, spot[1]] = made[a][lo:hi]
 
         wanted = list(range(groups))
         if final:
@@ -456,7 +457,7 @@
                     copy = pltpu.make_async_copy(
                         block.at[pl.ds(low, high - low), :],
                         restored.at[pl.ds(low, high - low), pl.ds(LANE * k, LANE)],
-                        refs[-1].at[len(leaving)],
+                        semaphores.at[len(leaving)],
                     )
                     copy.start()
                     leaving.append(copy)
@@ -470,27 +471,24 @@
     nz = target.shape[1] * SUB * LANE // (slab + 2 * halo)
     width = padded_to(slab + 2 * halo, SUB)
     vmem = pl.BlockSpec(memory_space=pltpu.VMEM)
+    dual_shapes = [(ny + framed, width, nz) for framed in (0, 2, 0)]
+    scratch_shapes = [pltpu.VMEM((ny + 2, width, nz), f32), pltpu.VMEM((ny, width, nz), f32)]
     if last:
         out_shape = jax.ShapeDtypeStruct((slab * ny, nz), f32)
         out_specs = pl.BlockSpec(memory_space=pltpu.HBM)
+        scratch_shapes += [pltpu.VMEM((slab * ny, LANE), f32)] * (nz // LANE)
+        scratch_shapes += [pltpu.VMEM(shape, f32) for shape in dual_shapes]
+        scratch_shapes.append(pltpu.SemaphoreType.DMA((nz // LANE * width // SUB,)))
     else:
-        kept = jax.ShapeDtypeStruct((ny, slab + 2 * HALO_LAST, nz), f32)
-        out_shape = [jax.ShapeDtypeStruct((ny, slab, nz), f32), kept, kept, kept]
+        out_shape = [jax.ShapeDtypeStruct((ny, slab, nz), f32)]
+        out_shape += [jax.ShapeDtypeStruct(shape, f32) for shape in dual_shapes]
         out_specs = [vmem] * 4
     return pl.pallas_call(
         functools.partial(passes_kernel, first, last, halo, slab, nx),
         in_specs=[vmem] * (1 + len(duals)),
         out_specs=out_specs,
         out_shape=out_shape,
-        scratch_shapes=[
-            pltpu.VMEM((ny + 2, width, nz), f32),
-            pltpu.VMEM((ny, width, nz), f32),
-            pltpu.VMEM((ny, width, nz), f32),
-            pltpu.VMEM((ny + 2, width, nz), f32),
-            pltpu.VMEM((ny, width, nz), f32),
-        ]
-        + [pltpu.VMEM((slab * ny, LANE), f32)] * (nz // LANE if last else 0)
-        + [pltpu.SemaphoreType.DMA((nz // LANE * width // SUB,))] * last,
+        scratch_shapes=scratch_shapes,
         compiler_params=pltpu.CompilerParams(vmem_limit_bytes=40 * MIB),
         cost_estimate=pl.CostEstimate(
             flops=60 * PASSES * ny * width * nz,
@@ -509,14 +507,14 @@
     devices = lax.axis_size("gy")
     rows = ny // devices
     nx = slab * devices
-    tables = [jnp.asarray(table) for table in (z_table(nz),) + x_tables(nx)]
+    tables = [jnp.asarray(table) for table in (z_table(nz), x_tables(nx))]
     cells = exchange(turn(observed).reshape(devices, rows, slab, nz))
-    weights = make_weights(tf_table, tilt_index, wedge, nx, nz)
+    both_data, prior = make_weights(tf_table, tilt_index, wedge, nx, nz)
     duals, kept = (), ()
     for outer in range(OUTER):
         first, last = outer == 0, outer == OUTER - 1
         halo = HALO_LAST if last else HALO_FIRST
-        made = run_filter(first, halo, cells, tables, weights, kept)
+        made = run_filter(first, halo, cells, tables, both_data if first else prior, kept)
         kept = made[1:]
         windows = exchange(made[0])
         target = windows.reshape((ny,) + windows.shape[2:])

time: 151 us -> 152 us (level)
    unnamed x20 -> x16, local copies, waits for them, and re-layouts: 4.62 us -> 4.76 us
where the time goes in v3:
time: 152 us; the launch traced here: 149 us
  blocking collectives  97.3 us (64%)
  Pallas kernels  20.7 us (14%)
  waiting for transfers between devices  19.7 us (13%)
  starting transfers between devices  6.44 us (4%)
  local copies, waits for them, and re-layouts  4.79 us (3%)
    all_to_all x3, blocking collectives, exchange(): return lax.all_to_all(blocks, 'gy', split_axis=0, concat_axis=0, tiled=True)  97.3 us
    all_to_all x1, waiting for transfers between devices, exchange(): return lax.all_to_all(blocks, 'gy', split_axis=0, concat_axis=0, tiled=True)  19.7 us
    pallas_call x2, Pallas kernels, run_passes(): pl.pallas_call(functools.partial(passes_kernel, first, last, halo, slab,...  10 us
    all_to_all x1, starting transfers between devices, exchange(): return lax.all_to_all(blocks, 'gy', split_axis=0, concat_axis=0, tiled=True)  6.44 us
    pallas_call x2, Pallas kernels, run_filter(): pl.pallas_call(functools.partial(filter_kernel, first, halo, slab), in_sp...  5.45 us
    unnamed x16, local copies, waits for them, and re-layouts  4.76 us
  transfers between devices with their start and end apart: 1, of which 1 were waited for; matrix products, arithmetic and copies ran while one was open for 0% of the time, Pallas kernels for 2%

profile of v3, /device:TPU:8, one launch (start us, length us, event | category | flops | bytes accessed | tf_op | source)
XLA Modules:
  0.0 149.3 jit_solution(8395188077392375984)
XLA Ops:
  0.0 2.2 %shard_map.64 = f32[16,64,256]{2,1,0:T(8,128)} custom-call(f32[1024,256]{1,0:T(8,128)} %bitcast.12), custom_call_target="tpu_custom_call" | custom-call | bytes 2097152 | tf_op jit(solution)/shard_map/pallas_call | solution.py:177
  2.2 0.0 copy-start.6
  2.2 0.0 copy-start.7
  2.2 0.0 copy-start
  2.3 6.4 %all-to-all-start = ((f32[16,1,64,256]{3,2,1,0:T(8,128)}), f32[16,1,64,256]{3,2,1,0:T(8,128)S(1)}, u32[]{:S(2)}, u32[]{:S(2)}) async-start(f32[16,1,64,256]{3,2,1,0:T(8,128)} %bitcast.11), calls=%async_computation | async-start | bytes 2097152 | tf_op jit(solution)/shard_map/all_to_all | solution.py:502
  8.7 0.0 copy-done.6
  8.7 0.0 copy-done.7
  8.7 0.1 fusion
  8.8 0.0 copy-done
  8.8 0.0 copy-start.3
  8.8 3.0 %shard_map.65 = (f32[2,1024,256]{2,1,0:T(8,128)S(1)}, f32[1024,256]{1,0:T(8,128)S(1)}) custom-call(f32[16]{0:T(128)S(1)} %copy-done, bf16[256,640]{1,0:T(8,128)(2,1)S(1)} %pad.5.code_ref), custom_call_target="tpu_custom_call" | custom-call | flops 15728640000 | bytes 2097152 | tf_op jit(solution)/shard_map/pallas_call | solution.py:110
  11.9 0.0 copy-start.4
  11.9 1.3 copy-done.4
  13.2 19.7 %all-to-all-done.refs_0_ = f32[16,1,64,256]{3,2,1,0:T(8,128)S(1)} async-done(((f32[16,1,64,256]{3,2,1,0:T(8,128)}), f32[16,1,64,256]{3,2,1,0:T(8,128)S(1)}, u32[]{:S(2)}, u32[]{:S(2)}) %all-to-all-start) | async-done | bytes 1048608 | tf_op jit(solution)/shard_map/all_to_all | solution.py:502
  32.9 0.0 copy-done.3
  32.9 0.0 copy-start.1
  32.9 1.8 %copy-done.1 = bf16[2,11,256,256]{3,2,1,0:T(8,128)(2,1)S(1)} copy-done((bf16[2,11,256,256]{3,2,1,0:T(8,128)(2,1)S(1)}, bf16[2,11,256,256]{3,2,1,0:T(8,128)(2,1)}, u32[]{:S(2)}) %copy-start.1) | copy-done | bytes 2883608
  34.7 0.0 copy-start.5
  34.7 1.6 %copy-done.5 = f32[2,1024,256]{2,1,0:T(8,128)S(1)} copy-done((f32[2,1024,256]{2,1,0:T(8,128)S(1)}, f32[2,1024,256]{2,1,0:T(8,128)}, u32[]{:S(2)}) %copy-start.5) | copy-done | bytes 2097176
  36.3 2.7 %shard_map.66 = (f32[16,1,19,8,128]{4,3,2,1,0:T(8,128)S(1)}, f32[1,1024,256]{2,1,0:T(8,128)S(1)}) custom-call(f32[16,1,64,256]{3,2,1,0:T(8,128)S(1)} %all-to-all-done.refs_0_, bf16[2,256,256]{2,1,0:T(8,128)(2,1)S(1)} %copy-done.3, bf16[2,11,256,256]{3,2,1,0:T(8,128)(2,1)S(1)} %copy-done.1, f32[2,1024,256]{2,1,0:T(8,128)S(1)} %copy-done.5), custom_call_target="tpu_custom_call" | custom-call | flops 2415919104 | bytes 2097152 | tf_op jit(solution)/shard_map/pallas_call | solution.py:273
  39.1 34.9 %all_to_all.20 = f32[16,1,19,8,128]{4,3,2,1,0:T(8,128)S(1)} all-to-all(f32[16,1,19,8,128]{4,3,2,1,0:T(8,128)S(1)} %get-tuple-element.14), channel_id=1, replica_groups=mesh['groups'=2,'gy'=16] {'gy'}, dimensions={0} | all-to-all | bytes 2490368 | tf_op jit(solution)/shard_map/all_to_all | solution.py:502
  74.0 0.0 copy-start.2
  74.0 4.2 %shard_map.67 = (f32[16,64,256]{2,1,0:T(8,128)S(1)}, f32[16,80,256]{2,1,0:T(8,128)S(1)}, f32[18,80,256]{2,1,0:T(8,128)S(1)}, f32[16,80,256]{2,1,0:T(8,128)S(1)}) custom-call(f32[16,19,8,128]{3,2,1,0:T(8,128)S(1)} %bitcast.8), custom_call_target="tpu_custom_call" | custom-call | flops 39321600 | bytes 10485760 | tf_op jit(solution)/shard_map/pallas_call | solution.py:486
  78.2 29.2 %all_to_all.21.refs_0_ = f32[16,1,64,256]{3,2,1,0:T(8,128)S(1)} all-to-all(f32[16,1,64,256]{3,2,1,0:T(8,128)S(1)} %bitcast.10), channel_id=1, replica_groups=mesh['groups'=2,'gy'=16] {'gy'}, dimensions={0} | all-to-all | bytes 2097152 | tf_op jit(solution)/shard_map/all_to_all | solution.py:502
  107.4 0.0 copy-done.2
  107.4 2.7 %shard_map.68 = f32[16,1,18,8,128]{4,3,2,1,0:T(8,128)S(1)} custom-call(f32[16,1,64,256]{3,2,1,0:T(8,128)S(1)} %all_to_all.21.refs_0_, bf16[2,256,256]{2,1,0:T(8,128)(2,1)S(1)} %copy-done.3, bf16[2,11,256,256]{3,2,1,0:T(8,128)(2,1)S(1)} %copy-done.2, f32[1024,256]{1,0:T(8,128)S(1)} %get-tuple-element.16.refs_3_, f32[1,1024,256]{2,1,0:T(8,128)S(1)} %get-tuple-element.17.refs_4_), custom_call_target="tpu_custom_call" | custom-call | flops 2415919104 | bytes 2097152 | tf_op jit(solution)/shard_map/pallas_call | solution.py:273
  110.1 33.2 %all_to_all.22 = f32[16,1,18,8,128]{4,3,2,1,0:T(8,128)S(1)} all-to-all(f32[16,1,18,8,128]{4,3,2,1,0:T(8,128)S(1)} %shard_map.68), channel_id=1, replica_groups=mesh['groups'=2,'gy'=16] {'gy'}, dimensions={0} | all-to-all | bytes 2359296 | tf_op jit(solution)/shard_map/all_to_all | solution.py:502
  143.3 5.9 %shard_map.69 = f32[1024,256]{1,0:T(8,128)} custom-call(f32[16,18,8,128]{3,2,1,0:T(8,128)S(1)} %bitcast.9, f32[16,80,256]{2,1,0:T(8,128)S(1)} %get-tuple-element.18.refs_0_, f32[18,80,256]{2,1,0:T(8,128)S(1)} %get-tuple-element.19.refs_1_, f32[16,80,256]{2,1,0:T(8,128)S(1)} %get-tuple-element.20.refs_2_), custom_call_target="tpu_custom_call" | custom-call | flops 35389440 | bytes 9437184 | tf_op jit(solution)/shard_map/pallas_call | solution.py:486
  (1 shorter events, 0.0 us)
Async XLA Ops:
  2.2 6.5 %copy-start.6 = (s32[513,129]{0,1:T(8,128)S(1)}, s32[513,129]{0,1:T(8,128)}, u32[]{:S(2)}) copy-start(s32[513,129]{0,1:T(8,128)} %param.8) | copy-start | bytes 794128
  2.2 6.5 %copy-start.7 = (s32[513,129]{0,1:T(8,128)S(1)}, s32[513,129]{0,1:T(8,128)}, u32[]{:S(2)}) copy-start(s32[513,129]{0,1:T(8,128)} %param.9) | copy-start | bytes 794128
  2.2 6.6 %copy-start = (f32[16]{0:T(128)S(1)}, f32[16]{0:T(128)}, u32[]{:S(2)}) copy-start(f32[16]{0:T(128)} %table_ref.1) | copy-start | bytes 196
  2.3 30.7 %all-to-all-start = ((f32[16,1,64,256]{3,2,1,0:T(8,128)}), f32[16,1,64,256]{3,2,1,0:T(8,128)S(1)}, u32[]{:S(2)}, u32[]{:S(2)}) async-start(f32[16,1,64,256]{3,2,1,0:T(8,128)} %bitcast.11), calls=%async_computation | async-start | bytes 2097152 | tf_op jit(solution)/shard_map/all_to_all | solution.py:502
  8.8 24.1 %copy-start.3 = (bf16[2,256,256]{2,1,0:T(8,128)(2,1)S(1)}, bf16[2,256,256]{2,1,0:T(8,128)(2,1)}, u32[]{:S(2)}) copy-start(bf16[2,256,256]{2,1,0:T(8,128)(2,1)} %constant.11.clone.refs_1_) | copy-start | bytes 786436
  11.9 1.3 copy-start.4
  32.9 1.8 %copy-start.1 = (bf16[2,11,256,256]{3,2,1,0:T(8,128)(2,1)S(1)}, bf16[2,11,256,256]{3,2,1,0:T(8,128)(2,1)}, u32[]{:S(2)}) copy-start(bf16[2,11,256,256]{3,2,1,0:T(8,128)(2,1)} %constant.12.clone.refs_2_) | copy-start | bytes 8650756
  34.7 1.6 %copy-start.5 = (f32[2,1024,256]{2,1,0:T(8,128)S(1)}, f32[2,1024,256]{2,1,0:T(8,128)}, u32[]{:S(2)}) copy-start(f32[2,1024,256]{2,1,0:T(8,128)} %copy-done.4) | copy-start | bytes 6291460
  74.0 33.4 %copy-start.2 = (bf16[2,11,256,256]{3,2,1,0:T(8,128)(2,1)S(1)}, bf16[2,11,256,256]{3,2,1,0:T(8,128)(2,1)}, u32[]{:S(2)}) copy-start(bf16[2,11,256,256]{3,2,1,0:T(8,128)(2,1)} %constant.12.clone.refs_2_) | copy-start | bytes 8650756

commit v4 on v2

--- a/solution.py
+++ b/solution.py
@@ -53,10 +53,12 @@
     half, quarter = length // 2, length // 4
     place = np.arange(half)
     fourth = cas(4 * place[:quarter], place[:quarter], length)
-    second = cas(4 * place[:quarter] + 2, place[:quarter], length)
-    odd = cas(2 * place + 1, place, length)
-    small = np.stack([halves(fourth), halves(second), halves(second.T)])
-    return small, np.stack([halves(odd), halves(odd.T)])
+    second = cas(4 * place[:quarter] + 2, 2 * place[:quarter] + 1, 2 * length)
+    odd = cas(2 * place + 1, 2 * place + 1, 2 * length)
+    blocks = [fourth, second]
+    for rows in (slice(0, quarter), slice(quarter, half)):
+        blocks += [odd[rows, :quarter], odd[rows, quarter:]]
+    return halves(np.stack(blocks))
 
 
 def kx_rows(length):
@@ -68,9 +70,8 @@
     return -(-length // unit) * unit
 
 
-def weights_kernel(nx, nz, levels, table_ref, code_ref, weights):
+def response_kernel(nx, nz, levels, table_ref, code_ref, response):
     heights, widths = code_ref.shape
-    scale = 1.0 / (nx * nz)
     kz = lax.broadcasted_iota(jnp.int32, (heights, nz), 1)
     kz = jnp.minimum(kz, nz - kz)
     pick_z = jnp.where(kz == lax.broadcasted_iota(jnp.int32, (heights, nz), 0), 1.0, 0.0)
@@ -88,29 +89,26 @@
                 preferred_element_type=f32,
             )
             spread = jnp.dot(tall.astype(bf16), pick_z, preferred_element_type=f32)
-            response = jnp.zeros_like(spread)
+            value = jnp.zeros_like(spread)
             for level in range(levels):
-                response = jnp.where(spread == level + 1.0, table_ref[level], response)
-            gain = scale / (response * response + 1.0)
-            rows = slice(base + top, base + top + tile)
-            weights[0, rows] = (UNIT * response) * gain
-            weights[1, rows] = gain
-
-
-def make_weights(tf_table, tilt_index, wedge, nx, nz):
+                value = jnp.where(spread == level + 1.0, table_ref[level], value)
+            response[base + top : base + top + tile] = value
+
+
+def make_response(tf_table, tilt_index, wedge, nx, nz):
     levels = tf_table.shape[0]
     code = jnp.where(wedge > 0, tilt_index + 1, 0).T
     extra = [(0, padded_to(size, LANE) - size) for size in code.shape]
     code = jnp.pad(code, extra).astype(bf16)
     vmem = pl.BlockSpec(memory_space=pltpu.VMEM)
     return pl.pallas_call(
-        functools.partial(weights_kernel, nx, nz, levels),
+        functools.partial(response_kernel, nx, nz, levels),
         in_specs=[pl.BlockSpec(memory_space=pltpu.SMEM), vmem],
         out_specs=vmem,
-        out_shape=jax.ShapeDtypeStruct((2, nx, nz), f32),
+        out_shape=jax.ShapeDtypeStruct((nx, nz), f32),
         compiler_params=pltpu.CompilerParams(vmem_limit_bytes=16 * MIB),
         cost_estimate=pl.CostEstimate(
-            flops=60000 * nx * nz, bytes_accessed=8 * nx * nz, transcendentals=0
+            flops=60000 * nx * nz, bytes_accessed=4 * nx * nz, transcendentals=0
         ),
     )(tf_table, code)
 
@@ -192,9 +190,9 @@
 
 
 def filter_kernel(first, halo, slab, *refs):
-    cells, ztab, small, odd, weights, refs = refs[:5] + (refs[5:],)
+    cells, ztab, xtab, weights, refs = refs[:4] + (refs[4:],)
     if first:
-        windows, kept, high, low, padded = refs
+        windows, kept, prior, high, low, padded = refs
     else:
         kept, windows, high, low, padded = refs
     devices, rows, _, nz = cells.shape
@@ -204,8 +202,8 @@
     blocks = nz // LANE
     ztable = (ztab[0], ztab[1])
 
-    def table(ref, i, rows=slice(None)):
-        return ref[i, 0, rows], ref[i, 1, rows]
+    def table(*places):
+        return [jnp.concatenate([xtab[part, i] for i in places], axis=1) for part in range(2)]
 
     def store(spot, value):
         high[spot], low[spot] = split(value)
@@ -224,21 +222,25 @@
         folded = (even[0] + even[1], even[0] - even[1], q[0] - q[2], q[1] - q[3])
         for spot, value in zip(parts, folded):
             store(spot, dot3(split(value), ztable))
-        waves = [dot3(table(small, i), load(folds[i])) for i in range(2)]
-        waves += [dot3(table(odd, 0, parts[i]), load(folds[2])) for i in range(2)]
+        waves = [dot3(table(i), load(folds[i])) for i in range(2)]
+        waves += [dot3(table(2 + 2 * i, 3 + 2 * i), load(folds[2])) for i in range(2)]
         for spot, wave in zip(parts, waves):
             if first:
-                seen = wave * weights[0, spot]
+                response = weights[spot]
+                gain = (1.0 / (nx * nz)) / (response * response + 1.0)
+                prior[spot] = gain
+                wave = wave * (UNIT * gain)
+                seen = wave * response
                 kept[r, spot] = seen
-                store(spot, seen + wave * (UNIT * weights[1, spot]))
+                store(spot, seen + wave)
             else:
-                store(spot, kept[r, spot] + wave * weights[1, spot])
+                store(spot, kept[r, spot] + wave * weights[spot])
         after = (halo + nx) // SUB * SUB
         padded[:SUB] = jnp.zeros((SUB, nz), f32)
         padded[after : after + 2 * SUB] = jnp.zeros((2 * SUB, nz), f32)
-        plus, minus = dot3(table(small, 0), load(folds[0])), dot3(table(small, 2), load(folds[1]))
+        plus, minus = dot3(table(0), load(folds[0])), dot3(table(1), load(folds[1]))
         for i, e in enumerate((plus + minus, plus - minus)):
-            o = dot3(table(odd, 1, parts[i]), load(folds[2]))
+            o = dot3(table(2 + 2 * i, 3 + 2 * i), load(folds[2]))
             for j, value in ((i, e + o), (i + 2, e - o)):
                 place = halo + j * quarter
                 padded[place : place + quarter] = dot3(split(value), ztable)
@@ -266,7 +268,10 @@
     tiles = window_tiles(slab + 2 * halo, nz)
     out_shape = [jax.ShapeDtypeStruct((devices, rows, tiles, SUB, LANE), f32)]
     if first:
-        out_shape.append(jax.ShapeDtypeStruct((rows, nx, nz), f32))
+        out_shape += [
+            jax.ShapeDtypeStruct((rows, nx, nz), f32),
+            jax.ShapeDtypeStruct((nx, nz), f32),
+        ]
     return pl.pallas_call(
         functools.partial(filter_kernel, first, halo, slab),
         in_specs=[vmem] * len(operands),
@@ -345,11 +350,24 @@
         shift = k * rest % SUB
         return pltpu.roll(tail, SUB - shift, 0) if shift else tail
 
+    inside = {}
+    for g in range(groups):
+        if SUB * g < halo or SUB * (g + 1) > width - halo:
+            place = origin + SUB * g + lax.broadcasted_iota(jnp.int32, (SUB, LANE), 0)
+            inside[g] = jnp.where((place >= 0) & (place < nx), 1.0, 0.0)
+
     def masked(value, g):
-        if SUB * g >= halo and SUB * (g + 1) <= width - halo:
-            return value
-        place = origin + SUB * g + lax.broadcasted_iota(jnp.int32, (SUB, LANE), 0)
-        return jnp.where((place >= 0) & (place < nx), value, 0.0)
+        return value * inside[g] if g in inside else value
+
+    def hand_on(which, y, g, k, value):
+        shift = halo - HALO_LAST
+        lo = max(0, shift - SUB * g)
+        hi = min(SUB, slab + 2 * HALO_LAST + shift - SUB * g)
+        if lo < hi:
+            rows = pl.ds(SUB * g + lo - shift, hi - lo)
+            duals_out[which][y, rows, pl.ds(LANE * k, LANE)] = value[lo:hi]
+
+    centre_groups = [g for g in range(groups) if SUB * (g + 1) > halo and SUB * g < width - halo]
 
     def at(g, k):
         return pl.ds(SUB * g, SUB), pl.ds(LANE * k, LANE)
@@ -397,17 +415,10 @@
                     dual_y[(y + 1,) + spot] = made[1]
                     dual_z[(y,) + spot] = made[2]
                     if final and not last:
-                        shift = halo - HALO_LAST
-                        lo = max(0, shift - SUB * g)
-                        hi = min(SUB, slab + 2 * HALO_LAST + shift - SUB * g)
-                        if lo < hi:
-                            rows = pl.ds(SUB * g + lo - shift, hi - lo)
-                            for a in range(3):
-                                duals_out[a][y, rows, spot[1]] = made[a][lo:hi]
-
-        wanted = list(range(groups))
-        if final:
-            wanted = [g for g in wanted if SUB * (g + 1) > halo and SUB * g < width - halo]
+                        for a in (0,) if g in centre_groups else (0, 1, 2):
+                            hand_on(a, y, g, k, made[a])
+
+        wanted = centre_groups if final else list(range(groups))
         column = COLUMN if final and last else len(wanted)
         for some in [wanted[i : i + column] for i in range(0, len(wanted), column)]:
 
@@ -424,7 +435,11 @@
                     for k in range(blocks):
                         spot = at(g, k)
                         along_y = dual_y[(y,) + spot] + dual_y[(y + 2,) + spot]
-                        centre = near[g][k] + dual_y[(y + 1,) + spot] + here[k]
+                        middle = dual_y[(y + 1,) + spot]
+                        if final and not last:
+                            hand_on(1, y, g, k, middle)
+                            hand_on(2, y, g, k, here[k])
+                        centre = near[g][k] + middle + here[k]
                         adjoint = columns[k][place] + along_y + along_z[k] - (centre + centre)
                         goal = goal_of(y, g, k)
                         if sweep == 0:
@@ -509,15 +524,16 @@
     devices = lax.axis_size("gy")
     rows = ny // devices
     nx = slab * devices
-    tables = [jnp.asarray(table) for table in (z_table(nz),) + x_tables(nx)]
+    tables = [jnp.asarray(table) for table in (z_table(nz), x_tables(nx))]
     cells = exchange(turn(observed).reshape(devices, rows, slab, nz))
-    weights = make_weights(tf_table, tilt_index, wedge, nx, nz)
+    weights = make_response(tf_table, tilt_index, wedge, nx, nz)
     duals, kept = (), ()
     for outer in range(OUTER):
         first, last = outer == 0, outer == OUTER - 1
         halo = HALO_LAST if last else HALO_FIRST
         made = run_filter(first, halo, cells, tables, weights, kept)
-        kept = made[1:]
+        if first:
+            kept, weights = (made[1],), made[2]
         windows = exchange(made[0])
         target = windows.reshape((ny,) + windows.shape[2:])
         made = run_passes(first, last, halo, slab, nx, target, duals)

time: 151 us -> 149 us (0.987)
  local copies, waits for them, and re-layouts: 4.65 us -> 2.79 us
    unnamed x20 -> x14, local copies, waits for them, and re-layouts: 4.62 us -> 2.76 us
where the time goes in v4:
time: 149 us; the launch traced here: 147 us
  blocking collectives  97.3 us (65%)
  Pallas kernels  20.1 us (13%)
  waiting for transfers between devices  19.9 us (13%)
  starting transfers between devices  6.44 us (4%)
  local copies, waits for them, and re-layouts  2.79 us (2%)
    all_to_all x3, blocking collectives, exchange(): return lax.all_to_all(blocks, 'gy', split_axis=0, concat_axis=0, tiled=True)  97.3 us
    all_to_all x1, waiting for transfers between devices, exchange(): return lax.all_to_all(blocks, 'gy', split_axis=0, concat_axis=0, tiled=True)  19.9 us
    pallas_call x2, Pallas kernels, run_passes(): pl.pallas_call(functools.partial(passes_kernel, first, last, halo, slab,...  9.66 us
    all_to_all x1, starting transfers between devices, exchange(): return lax.all_to_all(blocks, 'gy', split_axis=0, concat_axis=0, tiled=True)  6.44 us
    pallas_call x2, Pallas kernels, run_filter(): pl.pallas_call(functools.partial(filter_kernel, first, halo, slab), in_sp...  5.49 us
  transfers between devices with their start and end apart: 1, of which 1 were waited for; matrix products, arithmetic and copies ran while one was open for 0% of the time, Pallas kernels for 2%

profile of v4, /device:TPU:8, one launch (start us, length us, event | category | flops | bytes accessed | tf_op | source)
XLA Modules:
  0.0 146.6 jit_solution(16583776091241257256)
XLA Ops:
  0.0 2.2 %shard_map.64 = f32[16,64,256]{2,1,0:T(8,128)} custom-call(f32[1024,256]{1,0:T(8,128)} %bitcast.12), custom_call_target="tpu_custom_call" | custom-call | bytes 2097152 | tf_op jit(solution)/shard_map/pallas_call | solution.py:171
  2.2 0.0 copy-start.5
  2.2 0.0 copy-start.6
  2.2 6.4 %all-to-all-start = ((f32[16,1,64,256]{3,2,1,0:T(8,128)}), f32[16,1,64,256]{3,2,1,0:T(8,128)S(1)}, u32[]{:S(2)}, u32[]{:S(2)}) async-start(f32[16,1,64,256]{3,2,1,0:T(8,128)} %bitcast.11), calls=%async_computation | async-start | bytes 2097152 | tf_op jit(solution)/shard_map/all_to_all | solution.py:519
  8.7 0.0 copy-done.5
  8.7 0.0 copy-done.6
  8.7 0.0 copy-start
  8.7 0.1 fusion
  8.8 0.5 copy-done
  9.4 0.0 copy-start.1
  9.4 0.0 copy-start.2
  9.4 2.7 %shard_map.65.refs_3_ = f32[1024,256]{1,0:T(8,128)S(1)} custom-call(f32[16]{0:T(128)S(1)} %copy-done, bf16[256,640]{1,0:T(8,128)(2,1)S(1)} %pad.5.code_ref), custom_call_target="tpu_custom_call" | custom-call | flops 15728640000 | bytes 1048576 | tf_op jit(solution)/shard_map/pallas_call | solution.py:104
  12.1 0.0 copy-start.3
  12.1 1.0 copy-done.3
  13.1 19.9 %all-to-all-done.refs_0_ = f32[16,1,64,256]{3,2,1,0:T(8,128)S(1)} async-done(((f32[16,1,64,256]{3,2,1,0:T(8,128)}), f32[16,1,64,256]{3,2,1,0:T(8,128)S(1)}, u32[]{:S(2)}, u32[]{:S(2)}) %all-to-all-start) | async-done | bytes 1048608 | tf_op jit(solution)/shard_map/all_to_all | solution.py:519
  32.9 0.0 copy-done.1
  32.9 0.0 copy-done.2
  32.9 0.0 copy-start.4
  32.9 1.2 copy-done.4
  34.1 2.8 %shard_map.66 = (f32[16,1,19,8,128]{4,3,2,1,0:T(8,128)S(1)}, f32[1,1024,256]{2,1,0:T(8,128)S(1)}, f32[1024,256]{1,0:T(8,128)S(1)}) custom-call(f32[16,1,64,256]{3,2,1,0:T(8,128)S(1)} %all-to-all-done.refs_0_, bf16[2,256,256]{2,1,0:T(8,128)(2,1)S(1)} %copy-done.2, bf16[2,6,256,256]{3,2,1,0:T(8,128)(2,1)S(1)} %copy-done.1, f32[1024,256]{1,0:T(8,128)S(1)} %copy-done.4), custom_call_target="tpu_custom_call" | custom-call | flops 2415919104 | bytes 2097152 | tf_op jit(solution)/shard_map/pallas_call | solution.py:275
  36.9 34.9 %all_to_all.20 = f32[16,1,19,8,128]{4,3,2,1,0:T(8,128)S(1)} all-to-all(f32[16,1,19,8,128]{4,3,2,1,0:T(8,128)S(1)} %get-tuple-element.12), channel_id=1, replica_groups=mesh['groups'=2,'gy'=16] {'gy'}, dimensions={0} | all-to-all | bytes 2490368 | tf_op jit(solution)/shard_map/all_to_all | solution.py:519
  71.9 4.4 %shard_map.67 = (f32[16,64,256]{2,1,0:T(8,128)S(1)}, f32[16,72,256]{2,1,0:T(8,128)S(1)}, f32[16,72,256]{2,1,0:T(8,128)S(1)}, f32[16,72,256]{2,1,0:T(8,128)S(1)}) custom-call(f32[16,19,8,128]{3,2,1,0:T(8,128)S(1)} %bitcast.8), custom_call_target="tpu_custom_call" | custom-call | flops 39321600 | bytes 10485760 | tf_op jit(solution)/shard_map/pallas_call | solution.py:495
  76.3 29.2 %all_to_all.21.refs_0_ = f32[16,1,64,256]{3,2,1,0:T(8,128)S(1)} all-to-all(f32[16,1,64,256]{3,2,1,0:T(8,128)S(1)} %bitcast.10), channel_id=1, replica_groups=mesh['groups'=2,'gy'=16] {'gy'}, dimensions={0} | all-to-all | bytes 2097152 | tf_op jit(solution)/shard_map/all_to_all | solution.py:519
  105.5 2.7 %shard_map.68 = f32[16,1,18,8,128]{4,3,2,1,0:T(8,128)S(1)} custom-call(f32[16,1,64,256]{3,2,1,0:T(8,128)S(1)} %all_to_all.21.refs_0_, bf16[2,256,256]{2,1,0:T(8,128)(2,1)S(1)} %copy-done.2, bf16[2,6,256,256]{3,2,1,0:T(8,128)(2,1)S(1)} %copy-done.1, f32[1024,256]{1,0:T(8,128)S(1)} %get-tuple-element.14.refs_3_, f32[1,1024,256]{2,1,0:T(8,128)S(1)} %get-tuple-element.15.refs_4_), custom_call_target="tpu_custom_call" | custom-call | flops 2415919104 | bytes 2097152 | tf_op jit(solution)/shard_map/pallas_call | solution.py:275
  108.2 33.2 %all_to_all.22 = f32[16,1,18,8,128]{4,3,2,1,0:T(8,128)S(1)} all-to-all(f32[16,1,18,8,128]{4,3,2,1,0:T(8,128)S(1)} %shard_map.68), channel_id=1, replica_groups=mesh['groups'=2,'gy'=16] {'gy'}, dimensions={0} | all-to-all | bytes 2359296 | tf_op jit(solution)/shard_map/all_to_all | solution.py:519
  141.4 5.3 %shard_map.69 = f32[1024,256]{1,0:T(8,128)} custom-call(f32[16,18,8,128]{3,2,1,0:T(8,128)S(1)} %bitcast.9, f32[16,72,256]{2,1,0:T(8,128)S(1)} %get-tuple-element.16.refs_0_, f32[16,72,256]{2,1,0:T(8,128)S(1)} %get-tuple-element.17.refs_1_, f32[16,72,256]{2,1,0:T(8,128)S(1)} %get-tuple-element.18.refs_2_), custom_call_target="tpu_custom_call" | custom-call | flops 35389440 | bytes 9437184 | tf_op jit(solution)/shard_map/pallas_call | solution.py:495
  (1 shorter events, 0.0 us)
Async XLA Ops:
  2.2 6.5 %copy-start.5 = (s32[513,129]{0,1:T(8,128)S(1)}, s32[513,129]{0,1:T(8,128)}, u32[]{:S(2)}) copy-start(s32[513,129]{0,1:T(8,128)} %param.8) | copy-start | bytes 794128
  2.2 6.5 %copy-start.6 = (s32[513,129]{0,1:T(8,128)S(1)}, s32[513,129]{0,1:T(8,128)}, u32[]{:S(2)}) copy-start(s32[513,129]{0,1:T(8,128)} %param.9) | copy-start | bytes 794128
  2.2 30.7 %all-to-all-start = ((f32[16,1,64,256]{3,2,1,0:T(8,128)}), f32[16,1,64,256]{3,2,1,0:T(8,128)S(1)}, u32[]{:S(2)}, u32[]{:S(2)}) async-start(f32[16,1,64,256]{3,2,1,0:T(8,128)} %bitcast.11), calls=%async_computation | async-start | bytes 2097152 | tf_op jit(solution)/shard_map/all_to_all | solution.py:519
  8.7 0.7 copy-start
  9.4 23.6 %copy-start.1 = (bf16[2,6,256,256]{3,2,1,0:T(8,128)(2,1)S(1)}, bf16[2,6,256,256]{3,2,1,0:T(8,128)(2,1)}, u32[]{:S(2)}) copy-start(bf16[2,6,256,256]{3,2,1,0:T(8,128)(2,1)} %constant.12.clone.refs_2_) | copy-start | bytes 4718596
  9.4 23.6 %copy-start.2 = (bf16[2,256,256]{2,1,0:T(8,128)(2,1)S(1)}, bf16[2,256,256]{2,1,0:T(8,128)(2,1)}, u32[]{:S(2)}) copy-start(bf16[2,256,256]{2,1,0:T(8,128)(2,1)} %constant.11.clone.refs_1_) | copy-start | bytes 786436
  12.1 1.0 copy-start.3
  32.9 1.2 copy-start.4

commit v5 on v4

--- a/solution.py
+++ b/solution.py
@@ -21,8 +21,8 @@
 LANE = 128
 HALO_LAST = 2 * PASSES
 HALO_FIRST = HALO_LAST + 2 * PASSES - 2
-UNROLL = 8
-COLUMN = 3
+UNROLL = 16
+COLUMN = 4
 MIB = 1024 * 1024
 MOST_VMEM = 61 * MIB
 
@@ -190,17 +190,20 @@
 
 
 def filter_kernel(first, halo, slab, *refs):
-    cells, ztab, xtab, weights, refs = refs[:4] + (refs[4:],)
-    if first:
-        windows, kept, prior, high, low, padded = refs
-    else:
-        kept, windows, high, low, padded = refs
+    cells, weights, xtab, refs = refs[:3] + (refs[3:],)
     devices, rows, _, nz = cells.shape
     nx = devices * slab
     half, quarter = nx // 2, nx // 4
     width = slab + 2 * halo
     blocks = nz // LANE
-    ztable = (ztab[0], ztab[1])
+    if quarter == nz:
+        ztable = (xtab[0, 0], xtab[1, 0])
+    else:
+        ztable, refs = (refs[0][0], refs[0][1]), refs[1:]
+    if first:
+        windows, kept, prior, high, low, padded = refs
+    else:
+        kept, windows, high, low, padded = refs
 
     def table(*places):
         return [jnp.concatenate([xtab[part, i] for i in places], axis=1) for part in range(2)]
@@ -264,7 +267,7 @@
     devices, rows, slab, nz = cells.shape
     nx = devices * slab
     vmem = pl.BlockSpec(memory_space=pltpu.VMEM)
-    operands = [cells, *tables, weights, *kept]
+    operands = [cells, weights, *tables, *kept]
     tiles = window_tiles(slab + 2 * halo, nz)
     out_shape = [jax.ShapeDtypeStruct((devices, rows, tiles, SUB, LANE), f32)]
     if first:
@@ -524,7 +527,9 @@
     devices = lax.axis_size("gy")
     rows = ny // devices
     nx = slab * devices
-    tables = [jnp.asarray(table) for table in (z_table(nz), x_tables(nx))]
+    tables = [jnp.asarray(x_tables(nx))]
+    if nx != 4 * nz:
+        tables.append(jnp.asarray(z_table(nz)))
     cells = exchange(turn(observed).reshape(devices, rows, slab, nz))
     weights = make_response(tf_table, tilt_index, wedge, nx, nz)
     duals, kept = (), ()

time: 149 us -> 149 us (level)
  no operation moved by 1% of the time
where the time goes in v5:
time: 149 us; the launch traced here: 146 us
  blocking collectives  97.3 us (65%)
  waiting for transfers between devices  19.9 us (13%)
  Pallas kernels  19.5 us (13%)
  starting transfers between devices  6.44 us (4%)
  local copies, waits for them, and re-layouts  2.77 us (2%)
    all_to_all x3, blocking collectives, exchange(): return lax.all_to_all(blocks, 'gy', split_axis=0, concat_axis=0, tiled=True)  97.3 us
    all_to_all x1, waiting for transfers between devices, exchange(): return lax.all_to_all(blocks, 'gy', split_axis=0, concat_axis=0, tiled=True)  19.9 us
    pallas_call x2, Pallas kernels, run_passes(): pl.pallas_call(functools.partial(passes_kernel, first, last, halo, slab,...  9.08 us
    all_to_all x1, starting transfers between devices, exchange(): return lax.all_to_all(blocks, 'gy', split_axis=0, concat_axis=0, tiled=True)  6.44 us
    pallas_call x2, Pallas kernels, run_filter(): pl.pallas_call(functools.partial(filter_kernel, first, halo, slab), in_sp...  5.51 us
  transfers between devices with their start and end apart: 1, of which 1 were waited for; matrix products, arithmetic and copies ran while one was open for 0% of the time, Pallas kernels for 2%

profile of v5, /device:TPU:8, one launch (start us, length us, event | category | flops | bytes accessed | tf_op | source)
XLA Modules:
  0.0 146.2 jit_solution(16158050029718724159)
XLA Ops:
  0.0 2.2 %shard_map.55 = f32[16,64,256]{2,1,0:T(8,128)} custom-call(f32[1024,256]{1,0:T(8,128)} %bitcast.12), custom_call_target="tpu_custom_call" | custom-call | bytes 2097152 | tf_op jit(solution)/shard_map/pallas_call | solution.py:171
  2.2 0.0 copy-start.4
  2.2 0.0 copy-start.5
  2.2 6.4 %all-to-all-start = ((f32[16,1,64,256]{3,2,1,0:T(8,128)}), f32[16,1,64,256]{3,2,1,0:T(8,128)S(1)}, u32[]{:S(2)}, u32[]{:S(2)}) async-start(f32[16,1,64,256]{3,2,1,0:T(8,128)} %bitcast.11), calls=%async_computation | async-start | bytes 2097152 | tf_op jit(solution)/shard_map/all_to_all | solution.py:522
  8.7 0.0 copy-done.4
  8.7 0.0 copy-done.5
  8.7 0.0 copy-start
  8.7 0.1 fusion
  8.8 0.5 copy-done
  9.4 0.0 copy-start.1
  9.4 2.7 %shard_map.56.refs_1_ = f32[1024,256]{1,0:T(8,128)S(1)} custom-call(f32[16]{0:T(128)S(1)} %copy-done, bf16[256,640]{1,0:T(8,128)(2,1)S(1)} %pad.5.code_ref), custom_call_target="tpu_custom_call" | custom-call | flops 15728640000 | bytes 1048576 | tf_op jit(solution)/shard_map/pallas_call | solution.py:104
  12.1 0.0 copy-start.2
  12.1 1.0 copy-done.2
  13.0 19.9 %all-to-all-done.refs_0_ = f32[16,1,64,256]{3,2,1,0:T(8,128)S(1)} async-done(((f32[16,1,64,256]{3,2,1,0:T(8,128)}), f32[16,1,64,256]{3,2,1,0:T(8,128)S(1)}, u32[]{:S(2)}, u32[]{:S(2)}) %all-to-all-start) | async-done | bytes 1048608 | tf_op jit(solution)/shard_map/all_to_all | solution.py:522
  32.9 0.0 copy-done.1
  32.9 0.0 copy-start.3
  32.9 1.2 copy-done.3
  34.1 2.8 %shard_map.57 = (f32[16,1,19,8,128]{4,3,2,1,0:T(8,128)S(1)}, f32[1,1024,256]{2,1,0:T(8,128)S(1)}, f32[1024,256]{1,0:T(8,128)S(1)}) custom-call(f32[16,1,64,256]{3,2,1,0:T(8,128)S(1)} %all-to-all-done.refs_0_, f32[1024,256]{1,0:T(8,128)S(1)} %copy-done.3, bf16[2,6,256,256]{3,2,1,0:T(8,128)(2,1)S(1)} %copy-done.1), custom_call_target="tpu_custom_call" | custom-call | flops 2415919104 | bytes 2097152 | tf_op jit(solution)/shard_map/pallas_call | solution.py:278
  36.9 34.9 %all_to_all.20 = f32[16,1,19,8,128]{4,3,2,1,0:T(8,128)S(1)} all-to-all(f32[16,1,19,8,128]{4,3,2,1,0:T(8,128)S(1)} %get-tuple-element.12), channel_id=1, replica_groups=mesh['groups'=2,'gy'=16] {'gy'}, dimensions={0} | all-to-all | bytes 2490368 | tf_op jit(solution)/shard_map/all_to_all | solution.py:522
  71.9 4.2 %shard_map.58 = (f32[16,64,256]{2,1,0:T(8,128)S(1)}, f32[16,72,256]{2,1,0:T(8,128)S(1)}, f32[16,72,256]{2,1,0:T(8,128)S(1)}, f32[16,72,256]{2,1,0:T(8,128)S(1)}) custom-call(f32[16,19,8,128]{3,2,1,0:T(8,128)S(1)} %bitcast.8), custom_call_target="tpu_custom_call" | custom-call | flops 39321600 | bytes 10485760 | tf_op jit(solution)/shard_map/pallas_call | solution.py:498
  76.1 29.2 %all_to_all.21.refs_0_ = f32[16,1,64,256]{3,2,1,0:T(8,128)S(1)} all-to-all(f32[16,1,64,256]{3,2,1,0:T(8,128)S(1)} %bitcast.10), channel_id=1, replica_groups=mesh['groups'=2,'gy'=16] {'gy'}, dimensions={0} | all-to-all | bytes 2097152 | tf_op jit(solution)/shard_map/all_to_all | solution.py:522
  105.3 2.7 %shard_map.59 = f32[16,1,18,8,128]{4,3,2,1,0:T(8,128)S(1)} custom-call(f32[16,1,64,256]{3,2,1,0:T(8,128)S(1)} %all_to_all.21.refs_0_, f32[1024,256]{1,0:T(8,128)S(1)} %get-tuple-element.14.refs_1_, bf16[2,6,256,256]{3,2,1,0:T(8,128)(2,1)S(1)} %copy-done.1, f32[1,1024,256]{2,1,0:T(8,128)S(1)} %get-tuple-element.15.refs_3_), custom_call_target="tpu_custom_call" | custom-call | flops 2415919104 | bytes 2097152 | tf_op jit(solution)/shard_map/pallas_call | solution.py:278
  108.0 33.2 %all_to_all.22 = f32[16,1,18,8,128]{4,3,2,1,0:T(8,128)S(1)} all-to-all(f32[16,1,18,8,128]{4,3,2,1,0:T(8,128)S(1)} %shard_map.59), channel_id=1, replica_groups=mesh['groups'=2,'gy'=16] {'gy'}, dimensions={0} | all-to-all | bytes 2359296 | tf_op jit(solution)/shard_map/all_to_all | solution.py:522
  141.2 4.8 %shard_map.60 = f32[1024,256]{1,0:T(8,128)} custom-call(f32[16,18,8,128]{3,2,1,0:T(8,128)S(1)} %bitcast.9, f32[16,72,256]{2,1,0:T(8,128)S(1)} %get-tuple-element.16.refs_0_, f32[16,72,256]{2,1,0:T(8,128)S(1)} %get-tuple-element.17.refs_1_, f32[16,72,256]{2,1,0:T(8,128)S(1)} %get-tuple-element.18.refs_2_), custom_call_target="tpu_custom_call" | custom-call | flops 35389440 | bytes 9437184 | tf_op jit(solution)/shard_map/pallas_call | solution.py:498
  (1 shorter events, 0.0 us)
Async XLA Ops:
  2.2 6.5 %copy-start.4 = (s32[513,129]{0,1:T(8,128)S(1)}, s32[513,129]{0,1:T(8,128)}, u32[]{:S(2)}) copy-start(s32[513,129]{0,1:T(8,128)} %param.7) | copy-start | bytes 794128
  2.2 6.5 %copy-start.5 = (s32[513,129]{0,1:T(8,128)S(1)}, s32[513,129]{0,1:T(8,128)}, u32[]{:S(2)}) copy-start(s32[513,129]{0,1:T(8,128)} %param.8) | copy-start | bytes 794128
  2.2 30.7 %all-to-all-start = ((f32[16,1,64,256]{3,2,1,0:T(8,128)}), f32[16,1,64,256]{3,2,1,0:T(8,128)S(1)}, u32[]{:S(2)}, u32[]{:S(2)}) async-start(f32[16,1,64,256]{3,2,1,0:T(8,128)} %bitcast.11), calls=%async_computation | async-start | bytes 2097152 | tf_op jit(solution)/shard_map/all_to_all | solution.py:522
  8.7 0.7 copy-start
  9.4 23.6 %copy-start.1 = (bf16[2,6,256,256]{3,2,1,0:T(8,128)(2,1)S(1)}, bf16[2,6,256,256]{3,2,1,0:T(8,128)(2,1)}, u32[]{:S(2)}) copy-start(bf16[2,6,256,256]{3,2,1,0:T(8,128)(2,1)} %constant.9.clone.refs_2_) | copy-start | bytes 4718596
  12.1 1.0 copy-start.2
  32.9 1.2 copy-start.3

commit v6 on v5

--- a/solution.py
+++ b/solution.py
@@ -166,7 +166,7 @@
 
 def turn(observed):
     slab, ny, nz = observed.shape
-    planes = 2 * SUB if slab % (2 * SUB) == 0 else SUB
+    planes = SUB
     anywhere = pl.BlockSpec(memory_space=pltpu.HBM)
     return pl.pallas_call(
         functools.partial(turn_kernel, ny, planes),
@@ -189,10 +189,18 @@
     return width * nz // (SUB * LANE)
 
 
-def filter_kernel(first, halo, slab, *refs):
-    cells, weights, xtab, refs = refs[:3] + (refs[3:],)
-    devices, rows, _, nz = cells.shape
+def filter_kernel(first, opens, closes, halo, slab, *refs):
+    if opens:
+        cells, refs = refs[0], refs[1:]
+        devices, rows, _, nz = cells.shape
+    else:
+        arrived, refs = refs[0], refs[1:]
+        rows, nz = arrived.shape[0], arrived.shape[2]
+        devices = arrived.shape[1] // slab
     nx = devices * slab
+    if closes:
+        weights, refs = refs[0], refs[1:]
+    xtab, refs = refs[0], refs[1:]
     half, quarter = nx // 2, nx // 4
     width = slab + 2 * halo
     blocks = nz // LANE
@@ -200,7 +208,9 @@
         ztable = (xtab[0, 0], xtab[1, 0])
     else:
         ztable, refs = (refs[0][0], refs[0][1]), refs[1:]
-    if first:
+    if not closes:
+        leaving, high, low, padded = refs
+    elif first:
         windows, kept, prior, high, low, padded = refs
     else:
         kept, windows, high, low, padded = refs
@@ -217,16 +227,23 @@
     parts = [slice(i * quarter, (i + 1) * quarter) for i in range(4)]
     folds = [parts[0], parts[1], slice(half, nx)]
     for r in range(rows):
-        q = [
-            cells[i * devices // 4 : (i + 1) * devices // 4, r].reshape(quarter, nz)
-            for i in range(4)
-        ]
-        even = (q[0] + q[2], q[1] + q[3])
-        folded = (even[0] + even[1], even[0] - even[1], q[0] - q[2], q[1] - q[3])
-        for spot, value in zip(parts, folded):
-            store(spot, dot3(split(value), ztable))
-        waves = [dot3(table(i), load(folds[i])) for i in range(2)]
-        waves += [dot3(table(2 + 2 * i, 3 + 2 * i), load(folds[2])) for i in range(2)]
+        if opens:
+            q = [
+                cells[i * devices // 4 : (i + 1) * devices // 4, r].reshape(quarter, nz)
+                for i in range(4)
+            ]
+            even = (q[0] + q[2], q[1] + q[3])
+            folded = (even[0] + even[1], even[0] - even[1], q[0] - q[2], q[1] - q[3])
+            for spot, value in zip(parts, folded):
+                store(spot, dot3(split(value), ztable))
+            waves = [dot3(table(i), load(folds[i])) for i in range(2)]
+            waves += [dot3(table(2 + 2 * i, 3 + 2 * i), load(folds[2])) for i in range(2)]
+        else:
+            waves = [arrived[r, spot] for spot in parts]
+        if not closes:
+            for spot, wave in zip(parts, waves):
+                leaving[r, spot] = wave
+            continue
         for spot, wave in zip(parts, waves):
             if first:
                 response = weights[spot]
@@ -263,20 +280,25 @@
                 ]
 
 
-def run_filter(first, halo, cells, tables, weights, kept):
-    devices, rows, slab, nz = cells.shape
+def run_filter(first, opens, closes, halo, slab, source, weights, tables, kept):
+    if opens:
+        devices, rows, _, nz = source.shape
+    else:
+        devices, rows, nz = source.shape[1] // slab, source.shape[0], source.shape[2]
     nx = devices * slab
     vmem = pl.BlockSpec(memory_space=pltpu.VMEM)
-    operands = [cells, weights, *tables, *kept]
+    waves = jax.ShapeDtypeStruct((rows, nx, nz), f32)
     tiles = window_tiles(slab + 2 * halo, nz)
-    out_shape = [jax.ShapeDtypeStruct((devices, rows, tiles, SUB, LANE), f32)]
-    if first:
-        out_shape += [
-            jax.ShapeDtypeStruct((rows, nx, nz), f32),
-            jax.ShapeDtypeStruct((nx, nz), f32),
-        ]
+    if closes:
+        operands = [source, weights, *tables, *kept]
+        out_shape = [jax.ShapeDtypeStruct((devices, rows, tiles, SUB, LANE), f32)]
+        if first:
+            out_shape += [waves, jax.ShapeDtypeStruct((nx, nz), f32)]
+    else:
+        operands, out_shape = [source, *tables], [waves]
+    share = (opens + closes) / 2
     return pl.pallas_call(
-        functools.partial(filter_kernel, first, halo, slab),
+        functools.partial(filter_kernel, first, opens, closes, halo, slab),
         in_specs=[vmem] * len(operands),
         out_specs=[vmem] * len(out_shape),
         out_shape=out_shape,
@@ -287,7 +309,7 @@
         ],
         compiler_params=pltpu.CompilerParams(vmem_limit_bytes=24 * MIB),
         cost_estimate=pl.CostEstimate(
-            flops=6 * rows * nx * nz * (2 * nz + nx),
+            flops=int(share * 6 * rows * nx * nz * (2 * nz + nx)),
             bytes_accessed=8 * rows * nx * nz,
             transcendentals=0,
         ),
@@ -320,6 +342,17 @@
         jnp.where(row == SUB - 1, up[g + 1], up[g]) + jnp.where(row == 0, down[g - 1], down[g])
         for g in range(1, len(groups) - 1)
     ]
+
+
+def each_plane(count):
+    def run(body):
+        if count <= UNROLL:
+            for y in range(count):
+                body(y)
+        else:
+            pl.loop(0, count, unroll=UNROLL)(body)
+
+    return run
 
 
 def passes_kernel(first, last, halo, slab, nx, target, *refs):
@@ -380,26 +413,34 @@
         lead[plane] = empty
         dual_y[plane] = empty
 
-    @pl.loop(0, ny, unroll=UNROLL)
-    def _(y):
-        for g in range(groups):
-            for k in range(blocks):
-                lead[(y + 1,) + at(g, k)] = goal_of(y, g, k)
+    written_out = ny <= UNROLL
+    if not written_out:
+
+        @each_plane(ny)
+        def _(y):
+            for g in range(groups):
+                for k in range(blocks):
+                    lead[(y + 1,) + at(g, k)] = goal_of(y, g, k)
+
+    def lead_of(sweep, y, g, k):
+        if sweep == 0 and written_out:
+            return goal_of(y, g, k) if 0 <= y < ny else jnp.zeros((SUB, LANE), f32)
+        return lead[(y + 1,) + at(g, k)]
 
     leaving = []
     for sweep in range(PASSES):
         final = sweep == PASSES - 1
 
-        @pl.loop(0, ny, unroll=UNROLL)
+        @each_plane(ny)
         def _(y):
-            here = [[lead[(y + 1,) + at(g, k)] for k in range(blocks)] for g in range(groups)]
+            here = [[lead_of(sweep, y, g, k) for k in range(blocks)] for g in range(groups)]
             columns = [row_sums([here[g][k] for g in range(groups)]) for k in range(blocks)]
             for g in range(groups):
                 along_z = lane_sums(here[g])
                 for k in range(blocks):
                     spot = at(g, k)
                     twice = here[g][k] + here[g][k]
-                    along_y = lead[(y,) + spot] + lead[(y + 2,) + spot]
+                    along_y = lead_of(sweep, y - 1, g, k) + lead_of(sweep, y + 1, g, k)
                     raised = [columns[k][g] - twice, along_y - twice, along_z[k] - twice]
                     if sweep > 0:
                         before = [dual_x[(y,) + spot], dual_y[(y + 1,) + spot], dual_z[(y,) + spot]]
@@ -425,7 +466,7 @@
         column = COLUMN if final and last else len(wanted)
         for some in [wanted[i : i + column] for i in range(0, len(wanted), column)]:
 
-            @pl.loop(0, ny, unroll=UNROLL)
+            @each_plane(ny)
             def _(y):
                 around = [some[0] - 1] + some + [some[-1] + 1]
                 near = {
@@ -536,7 +577,9 @@
     for outer in range(OUTER):
         first, last = outer == 0, outer == OUTER - 1
         halo = HALO_LAST if last else HALO_FIRST
-        made = run_filter(first, halo, cells, tables, weights, kept)
+        if first:
+            (cells,) = run_filter(True, True, False, halo, slab, cells, None, tables, kept)
+        made = run_filter(first, not first, True, halo, slab, cells, weights, tables, kept)
         if first:
             kept, weights = (made[1],), made[2]
         windows = exchange(made[0])

time: 149 us -> 148 us (level)
    pallas_call x2 -> x3, Pallas kernels: 5.51 us -> 5.72 us  [run_filter(): pl.pallas_call(functools.partial(filter_kernel, first, opens, closes, hal...]
where the time goes in v6:
time: 148 us; the launch traced here: 145 us
  blocking collectives  97.3 us (66%)
  waiting for transfers between devices  19.9 us (13%)
  Pallas kernels  19.8 us (13%)
  starting transfers between devices  6.44 us (4%)
  local copies, waits for them, and re-layouts  1.57 us (1%)
    all_to_all x3, blocking collectives, exchange(): return lax.all_to_all(blocks, 'gy', split_axis=0, concat_axis=0, tiled=True)  97.3 us
    all_to_all x1, waiting for transfers between devices, exchange(): return lax.all_to_all(blocks, 'gy', split_axis=0, concat_axis=0, tiled=True)  19.9 us
    pallas_call x2, Pallas kernels, run_passes(): pl.pallas_call(functools.partial(passes_kernel, first, last, halo, slab,...  9.11 us
    all_to_all x1, starting transfers between devices, exchange(): return lax.all_to_all(blocks, 'gy', split_axis=0, concat_axis=0, tiled=True)  6.44 us
    pallas_call x3, Pallas kernels, run_filter(): pl.pallas_call(functools.partial(filter_kernel, first, opens, closes, hal...  5.72 us
  transfers between devices with their start and end apart: 1, of which 1 were waited for; matrix products, arithmetic and copies ran while one was open for 0% of the time, Pallas kernels for 2%

profile of v6, /device:TPU:8, one launch (start us, length us, event | category | flops | bytes accessed | tf_op | source)
XLA Modules:
  0.0 145.3 jit_solution(10465438950599930754)
XLA Ops:
  0.0 2.2 %shard_map.55 = f32[16,64,256]{2,1,0:T(8,128)} custom-call(f32[1024,256]{1,0:T(8,128)} %bitcast.12), custom_call_target="tpu_custom_call" | custom-call | bytes 2097152 | tf_op jit(solution)/shard_map/pallas_call | solution.py:171
  2.2 0.0 copy-start.4
  2.3 0.0 copy-start.5
  2.3 6.4 %all-to-all-start = ((f32[16,1,64,256]{3,2,1,0:T(8,128)}), f32[16,1,64,256]{3,2,1,0:T(8,128)S(1)}, u32[]{:S(2)}, u32[]{:S(2)}) async-start(f32[16,1,64,256]{3,2,1,0:T(8,128)} %bitcast.11), calls=%async_computation | async-start | bytes 2097152 | tf_op jit(solution)/shard_map/all_to_all | solution.py:563
  8.7 0.0 copy-done.4
  8.7 0.0 copy-done.5
  8.7 0.0 copy-start
  8.7 0.1 fusion
  8.8 0.5 copy-done
  9.4 0.0 copy-start.1
  9.4 2.7 %shard_map.57.refs_1_ = f32[1024,256]{1,0:T(8,128)S(1)} custom-call(f32[16]{0:T(128)S(1)} %copy-done, bf16[256,640]{1,0:T(8,128)(2,1)S(1)} %pad.5.code_ref), custom_call_target="tpu_custom_call" | custom-call | flops 15728640000 | bytes 1048576 | tf_op jit(solution)/shard_map/pallas_call | solution.py:104
  12.1 0.0 copy-start.2
  12.1 1.0 copy-done.2
  13.1 19.9 %all-to-all-done.refs_0_ = f32[16,1,64,256]{3,2,1,0:T(8,128)S(1)} async-done(((f32[16,1,64,256]{3,2,1,0:T(8,128)}), f32[16,1,64,256]{3,2,1,0:T(8,128)S(1)}, u32[]{:S(2)}, u32[]{:S(2)}) %all-to-all-start) | async-done | bytes 1048608 | tf_op jit(solution)/shard_map/all_to_all | solution.py:563
  32.9 0.0 copy-done.1
  32.9 0.0 copy-start.3
  32.9 1.2 shard_map.56.refs_0_
  34.1 0.0 copy-done.3
  34.2 1.8 %shard_map.58 = (f32[16,1,19,8,128]{4,3,2,1,0:T(8,128)S(1)}, f32[1,1024,256]{2,1,0:T(8,128)S(1)}, f32[1024,256]{1,0:T(8,128)S(1)}) custom-call(f32[1,1024,256]{2,1,0:T(8,128)S(1)} %shard_map.56.refs_0_, f32[1024,256]{1,0:T(8,128)S(1)} %copy-done.3, bf16[2,6,256,256]{3,2,1,0:T(8,128)(2,1)S(1)} %copy-done.1), custom_call_target="tpu_custom_call" | custom-call | flops 1207959552 | bytes 2097152 | tf_op jit(solution)/shard_map/pallas_call | solution.py:300
  36.0 34.9 %all_to_all.20 = f32[16,1,19,8,128]{4,3,2,1,0:T(8,128)S(1)} all-to-all(f32[16,1,19,8,128]{4,3,2,1,0:T(8,128)S(1)} %get-tuple-element.12), channel_id=1, replica_groups=mesh['groups'=2,'gy'=16] {'gy'}, dimensions={0} | all-to-all | bytes 2490368 | tf_op jit(solution)/shard_map/all_to_all | solution.py:563
  70.9 4.2 %shard_map.59 = (f32[16,64,256]{2,1,0:T(8,128)S(1)}, f32[16,72,256]{2,1,0:T(8,128)S(1)}, f32[16,72,256]{2,1,0:T(8,128)S(1)}, f32[16,72,256]{2,1,0:T(8,128)S(1)}) custom-call(f32[16,19,8,128]{3,2,1,0:T(8,128)S(1)} %bitcast.8), custom_call_target="tpu_custom_call" | custom-call | flops 39321600 | bytes 10485760 | tf_op jit(solution)/shard_map/pallas_call | solution.py:539
  75.1 29.2 %all_to_all.21.refs_0_ = f32[16,1,64,256]{3,2,1,0:T(8,128)S(1)} all-to-all(f32[16,1,64,256]{3,2,1,0:T(8,128)S(1)} %bitcast.10), channel_id=1, replica_groups=mesh['groups'=2,'gy'=16] {'gy'}, dimensions={0} | all-to-all | bytes 2097152 | tf_op jit(solution)/shard_map/all_to_all | solution.py:563
  104.3 2.7 %shard_map.60 = f32[16,1,18,8,128]{4,3,2,1,0:T(8,128)S(1)} custom-call(f32[16,1,64,256]{3,2,1,0:T(8,128)S(1)} %all_to_all.21.refs_0_, f32[1024,256]{1,0:T(8,128)S(1)} %get-tuple-element.14.refs_1_, bf16[2,6,256,256]{3,2,1,0:T(8,128)(2,1)S(1)} %copy-done.1, f32[1,1024,256]{2,1,0:T(8,128)S(1)} %get-tuple-element.15.refs_3_), custom_call_target="tpu_custom_call" | custom-call | flops 2415919104 | bytes 2097152 | tf_op jit(solution)/shard_map/pallas_call | solution.py:300
  107.1 33.2 %all_to_all.22 = f32[16,1,18,8,128]{4,3,2,1,0:T(8,128)S(1)} all-to-all(f32[16,1,18,8,128]{4,3,2,1,0:T(8,128)S(1)} %shard_map.60), channel_id=1, replica_groups=mesh['groups'=2,'gy'=16] {'gy'}, dimensions={0} | all-to-all | bytes 2359296 | tf_op jit(solution)/shard_map/all_to_all | solution.py:563
  140.3 4.9 %shard_map.61 = f32[1024,256]{1,0:T(8,128)} custom-call(f32[16,18,8,128]{3,2,1,0:T(8,128)S(1)} %bitcast.9, f32[16,72,256]{2,1,0:T(8,128)S(1)} %get-tuple-element.16.refs_0_, f32[16,72,256]{2,1,0:T(8,128)S(1)} %get-tuple-element.17.refs_1_, f32[16,72,256]{2,1,0:T(8,128)S(1)} %get-tuple-element.18.refs_2_), custom_call_target="tpu_custom_call" | custom-call | flops 35389440 | bytes 9437184 | tf_op jit(solution)/shard_map/pallas_call | solution.py:539
  (1 shorter events, 0.0 us)
Async XLA Ops:
  2.2 6.5 %copy-start.4 = (s32[513,129]{0,1:T(8,128)S(1)}, s32[513,129]{0,1:T(8,128)}, u32[]{:S(2)}) copy-start(s32[513,129]{0,1:T(8,128)} %param.7) | copy-start | bytes 794128
  2.3 6.5 %copy-start.5 = (s32[513,129]{0,1:T(8,128)S(1)}, s32[513,129]{0,1:T(8,128)}, u32[]{:S(2)}) copy-start(s32[513,129]{0,1:T(8,128)} %param.8) | copy-start | bytes 794128
  2.3 30.7 %all-to-all-start = ((f32[16,1,64,256]{3,2,1,0:T(8,128)}), f32[16,1,64,256]{3,2,1,0:T(8,128)S(1)}, u32[]{:S(2)}, u32[]{:S(2)}) async-start(f32[16,1,64,256]{3,2,1,0:T(8,128)} %bitcast.11), calls=%async_computation | async-start | bytes 2097152 | tf_op jit(solution)/shard_map/all_to_all | solution.py:563
  8.7 0.7 copy-start
  9.4 23.6 %copy-start.1 = (bf16[2,6,256,256]{3,2,1,0:T(8,128)(2,1)S(1)}, bf16[2,6,256,256]{3,2,1,0:T(8,128)(2,1)}, u32[]{:S(2)}) copy-start(bf16[2,6,256,256]{3,2,1,0:T(8,128)(2,1)} %constant.9.clone.refs_1_.refs_2_) | copy-start | bytes 4718596
  12.1 1.0 copy-start.2
  32.9 1.2 copy-start.3

commit v7 on v6

--- a/solution.py
+++ b/solution.py
@@ -153,12 +153,10 @@
     for step in range(steps):
         for copy in incoming[step]:
             copy.wait()
-        for y in range(ny):
-            for x in range(step * planes, (step + 1) * planes, SUB):
-                for k in range(blocks):
-                    placed[y, x : x + SUB, LANE * k : LANE * (k + 1)] = staged[k][
-                        pl.ds(x * ny + y, SUB, stride=ny), :
-                    ]
+        for x in range(step * planes, (step + 1) * planes, SUB):
+            for k in range(blocks):
+                block = staged[k][x * ny : (x + SUB) * ny].reshape(SUB, ny, LANE)
+                placed[:, x : x + SUB, LANE * k : LANE * (k + 1)] = jnp.swapaxes(block, 0, 1)
         outgoing[step].start()
     for copy in outgoing:
         copy.wait()
@@ -365,7 +363,8 @@
     else:
         current, duals_out, refs = refs[0], refs[1:4], refs[4:]
     lead, field, dual_x, dual_y, dual_z = refs[:5]
-    turned = refs[5:-1] if last else ()
+    if last:
+        placed, turned, semaphores = refs[5:]
     ny, _, nz = field.shape
     width = slab + 2 * halo
     groups = padded_to(width, SUB) // SUB
@@ -427,7 +426,7 @@
             return goal_of(y, g, k) if 0 <= y < ny else jnp.zeros((SUB, LANE), f32)
         return lead[(y + 1,) + at(g, k)]
 
-    leaving = []
+    leaving, gone = [], 0
     for sweep in range(PASSES):
         final = sweep == PASSES - 1
 
@@ -504,21 +503,25 @@
                         hi = min(SUB, slab + halo - SUB * g)
                         x = SUB * g + lo - halo
                         if last:
-                            turned[k][pl.ds(x * ny + y, hi - lo, stride=ny), :] = updated[lo:hi]
+                            placed[y, pl.ds(x, hi - lo), spot[1]] = updated[lo:hi]
                         else:
                             current[y, pl.ds(x, hi - lo), spot[1]] = updated[lo:hi]
 
             if final and last:
-                low = max(0, SUB * some[0] - halo) * ny
-                high = min(slab, SUB * (some[-1] + 1) - halo) * ny
-                for k, block in enumerate(turned):
+                ready = min(slab, SUB * (some[-1] + 1) - halo) // SUB * SUB
+                for x in range(gone, ready, SUB):
+                    for k in range(blocks):
+                        lanes = pl.ds(LANE * k, LANE)
+                        block = jnp.swapaxes(placed[:, pl.ds(x, SUB), lanes], 0, 1)
+                        turned[pl.ds(x * ny, SUB * ny), lanes] = block.reshape(SUB * ny, LANE)
+                if ready > gone:
+                    rows = pl.ds(gone * ny, (ready - gone) * ny)
                     copy = pltpu.make_async_copy(
-                        block.at[pl.ds(low, high - low), :],
-                        restored.at[pl.ds(low, high - low), pl.ds(LANE * k, LANE)],
-                        refs[-1].at[len(leaving)],
+                        turned.at[rows, :], restored.at[rows, :], semaphores.at[len(leaving)]
                     )
                     copy.start()
                     leaving.append(copy)
+                gone = ready
 
     for copy in leaving:
         copy.wait()
@@ -548,8 +551,12 @@
             pltpu.VMEM((ny + 2, width, nz), f32),
             pltpu.VMEM((ny, width, nz), f32),
         ]
-        + [pltpu.VMEM((slab * ny, LANE), f32)] * (nz // LANE if last else 0)
-        + [pltpu.SemaphoreType.DMA((nz // LANE * width // SUB,))] * last,
+        + [
+            pltpu.VMEM((ny, slab, nz), f32),
+            pltpu.VMEM((slab * ny, nz), f32),
+            pltpu.SemaphoreType.DMA((width // SUB,)),
+        ]
+        * last,
         compiler_params=pltpu.CompilerParams(vmem_limit_bytes=40 * MIB),
         cost_estimate=pl.CostEstimate(
             flops=60 * PASSES * ny * width * nz,

time: 148 us -> 148 us (level)
  no operation moved by 1% of the time
where the time goes in v7:
time: 148 us; the launch traced here: 145 us
  blocking collectives  97.3 us (66%)
  waiting for transfers between devices  19.9 us (13%)
  Pallas kernels  19.7 us (13%)
  starting transfers between devices  6.44 us (4%)
  local copies, waits for them, and re-layouts  1.57 us (1%)
    all_to_all x3, blocking collectives, exchange(): return lax.all_to_all(blocks, 'gy', split_axis=0, concat_axis=0, tiled=True)  97.3 us
    all_to_all x1, waiting for transfers between devices, exchange(): return lax.all_to_all(blocks, 'gy', split_axis=0, concat_axis=0, tiled=True)  19.9 us
    pallas_call x2, Pallas kernels, run_passes(): pl.pallas_call(functools.partial(passes_kernel, first, last, halo, slab,...  9.11 us
    all_to_all x1, starting transfers between devices, exchange(): return lax.all_to_all(blocks, 'gy', split_axis=0, concat_axis=0, tiled=True)  6.44 us
    pallas_call x3, Pallas kernels, run_filter(): pl.pallas_call(functools.partial(filter_kernel, first, opens, closes, hal...  5.72 us
  transfers between devices with their start and end apart: 1, of which 1 were waited for; matrix products, arithmetic and copies ran while one was open for 0% of the time, Pallas kernels for 2%

profile of v7, /device:TPU:8, one launch (start us, length us, event | category | flops | bytes accessed | tf_op | source)
XLA Modules:
  0.0 145.3 jit_solution(8775331161112342340)
XLA Ops:
  0.0 2.2 %shard_map.55 = f32[16,64,256]{2,1,0:T(8,128)} custom-call(f32[1024,256]{1,0:T(8,128)} %bitcast.12), custom_call_target="tpu_custom_call" | custom-call | bytes 2097152 | tf_op jit(solution)/shard_map/pallas_call | solution.py:169
  2.2 0.0 copy-start.4
  2.2 0.0 copy-start.5
  2.2 6.4 %all-to-all-start = ((f32[16,1,64,256]{3,2,1,0:T(8,128)}), f32[16,1,64,256]{3,2,1,0:T(8,128)S(1)}, u32[]{:S(2)}, u32[]{:S(2)}) async-start(f32[16,1,64,256]{3,2,1,0:T(8,128)} %bitcast.11), calls=%async_computation | async-start | bytes 2097152 | tf_op jit(solution)/shard_map/all_to_all | solution.py:570
  8.7 0.0 copy-done.4
  8.7 0.0 copy-done.5
  8.7 0.0 copy-start
  8.7 0.1 fusion
  8.8 0.5 copy-done
  9.4 0.0 copy-start.1
  9.4 2.7 %shard_map.57.refs_1_ = f32[1024,256]{1,0:T(8,128)S(1)} custom-call(f32[16]{0:T(128)S(1)} %copy-done, bf16[256,640]{1,0:T(8,128)(2,1)S(1)} %pad.5.code_ref), custom_call_target="tpu_custom_call" | custom-call | flops 15728640000 | bytes 1048576 | tf_op jit(solution)/shard_map/pallas_call | solution.py:104
  12.1 0.0 copy-start.2
  12.1 1.0 copy-done.2
  13.0 19.9 %all-to-all-done.refs_0_ = f32[16,1,64,256]{3,2,1,0:T(8,128)S(1)} async-done(((f32[16,1,64,256]{3,2,1,0:T(8,128)}), f32[16,1,64,256]{3,2,1,0:T(8,128)S(1)}, u32[]{:S(2)}, u32[]{:S(2)}) %all-to-all-start) | async-done | bytes 1048608 | tf_op jit(solution)/shard_map/all_to_all | solution.py:570
  32.9 0.0 copy-done.1
  32.9 0.0 copy-start.3
  32.9 1.2 shard_map.56.refs_0_
  34.1 0.0 copy-done.3
  34.1 1.8 %shard_map.58 = (f32[16,1,19,8,128]{4,3,2,1,0:T(8,128)S(1)}, f32[1,1024,256]{2,1,0:T(8,128)S(1)}, f32[1024,256]{1,0:T(8,128)S(1)}) custom-call(f32[1,1024,256]{2,1,0:T(8,128)S(1)} %shard_map.56.refs_0_, f32[1024,256]{1,0:T(8,128)S(1)} %copy-done.3, bf16[2,6,256,256]{3,2,1,0:T(8,128)(2,1)S(1)} %copy-done.1), custom_call_target="tpu_custom_call" | custom-call | flops 1207959552 | bytes 2097152 | tf_op jit(solution)/shard_map/pallas_call | solution.py:298
  35.9 34.9 %all_to_all.20 = f32[16,1,19,8,128]{4,3,2,1,0:T(8,128)S(1)} all-to-all(f32[16,1,19,8,128]{4,3,2,1,0:T(8,128)S(1)} %get-tuple-element.12), channel_id=1, replica_groups=mesh['groups'=2,'gy'=16] {'gy'}, dimensions={0} | all-to-all | bytes 2490368 | tf_op jit(solution)/shard_map/all_to_all | solution.py:570
  70.9 4.2 %shard_map.59 = (f32[16,64,256]{2,1,0:T(8,128)S(1)}, f32[16,72,256]{2,1,0:T(8,128)S(1)}, f32[16,72,256]{2,1,0:T(8,128)S(1)}, f32[16,72,256]{2,1,0:T(8,128)S(1)}) custom-call(f32[16,19,8,128]{3,2,1,0:T(8,128)S(1)} %bitcast.8), custom_call_target="tpu_custom_call" | custom-call | flops 39321600 | bytes 10485760 | tf_op jit(solution)/shard_map/pallas_call | solution.py:542
  75.1 29.2 %all_to_all.21.refs_0_ = f32[16,1,64,256]{3,2,1,0:T(8,128)S(1)} all-to-all(f32[16,1,64,256]{3,2,1,0:T(8,128)S(1)} %bitcast.10), channel_id=1, replica_groups=mesh['groups'=2,'gy'=16] {'gy'}, dimensions={0} | all-to-all | bytes 2097152 | tf_op jit(solution)/shard_map/all_to_all | solution.py:570
  104.3 2.7 %shard_map.60 = f32[16,1,18,8,128]{4,3,2,1,0:T(8,128)S(1)} custom-call(f32[16,1,64,256]{3,2,1,0:T(8,128)S(1)} %all_to_all.21.refs_0_, f32[1024,256]{1,0:T(8,128)S(1)} %get-tuple-element.14.refs_1_, bf16[2,6,256,256]{3,2,1,0:T(8,128)(2,1)S(1)} %copy-done.1, f32[1,1024,256]{2,1,0:T(8,128)S(1)} %get-tuple-element.15.refs_3_), custom_call_target="tpu_custom_call" | custom-call | flops 2415919104 | bytes 2097152 | tf_op jit(solution)/shard_map/pallas_call | solution.py:298
  107.0 33.2 %all_to_all.22 = f32[16,1,18,8,128]{4,3,2,1,0:T(8,128)S(1)} all-to-all(f32[16,1,18,8,128]{4,3,2,1,0:T(8,128)S(1)} %shard_map.60), channel_id=1, replica_groups=mesh['groups'=2,'gy'=16] {'gy'}, dimensions={0} | all-to-all | bytes 2359296 | tf_op jit(solution)/shard_map/all_to_all | solution.py:570
  140.2 4.9 %shard_map.61 = f32[1024,256]{1,0:T(8,128)} custom-call(f32[16,18,8,128]{3,2,1,0:T(8,128)S(1)} %bitcast.9, f32[16,72,256]{2,1,0:T(8,128)S(1)} %get-tuple-element.16.refs_0_, f32[16,72,256]{2,1,0:T(8,128)S(1)} %get-tuple-element.17.refs_1_, f32[16,72,256]{2,1,0:T(8,128)S(1)} %get-tuple-element.18.refs_2_), custom_call_target="tpu_custom_call" | custom-call | flops 35389440 | bytes 9437184 | tf_op jit(solution)/shard_map/pallas_call | solution.py:542
  (1 shorter events, 0.0 us)
Async XLA Ops:
  2.2 6.5 %copy-start.4 = (s32[513,129]{0,1:T(8,128)S(1)}, s32[513,129]{0,1:T(8,128)}, u32[]{:S(2)}) copy-start(s32[513,129]{0,1:T(8,128)} %param.7) | copy-start | bytes 794128
  2.2 6.5 %copy-start.5 = (s32[513,129]{0,1:T(8,128)S(1)}, s32[513,129]{0,1:T(8,128)}, u32[]{:S(2)}) copy-start(s32[513,129]{0,1:T(8,128)} %param.8) | copy-start | bytes 794128
  2.2 30.7 %all-to-all-start = ((f32[16,1,64,256]{3,2,1,0:T(8,128)}), f32[16,1,64,256]{3,2,1,0:T(8,128)S(1)}, u32[]{:S(2)}, u32[]{:S(2)}) async-start(f32[16,1,64,256]{3,2,1,0:T(8,128)} %bitcast.11), calls=%async_computation | async-start | bytes 2097152 | tf_op jit(solution)/shard_map/all_to_all | solution.py:570
  8.7 0.7 copy-start
  9.4 23.6 %copy-start.1 = (bf16[2,6,256,256]{3,2,1,0:T(8,128)(2,1)S(1)}, bf16[2,6,256,256]{3,2,1,0:T(8,128)(2,1)}, u32[]{:S(2)}) copy-start(bf16[2,6,256,256]{3,2,1,0:T(8,128)(2,1)} %constant.9.clone.refs_1_.refs_2_) | copy-start | bytes 4718596
  12.1 1.0 copy-start.2
  32.9 1.2 copy-start.3

commit v8 on v7

--- a/solution.py
+++ b/solution.py
@@ -125,38 +125,34 @@
 
 
 def turn_kernel(ny, planes, cells, turned, staged, placed, semaphores):
-    blocks = len(staged)
-    steps = placed.shape[1] // planes
+    slab, nz = placed.shape[1:]
+    steps = slab // planes
     rows = planes * ny
     incoming = [
-        [
-            pltpu.make_async_copy(
-                cells.at[pl.ds(step * rows, rows), pl.ds(LANE * k, LANE)],
-                staged[k].at[pl.ds(step * rows, rows), :],
-                semaphores.at[0, step, k],
-            )
-            for k in range(blocks)
-        ]
+        pltpu.make_async_copy(
+            cells.at[pl.ds(step * rows, rows), :],
+            staged.at[pl.ds(step * rows, rows), :],
+            semaphores.at[0, step],
+        )
         for step in range(steps)
     ]
     outgoing = [
         pltpu.make_async_copy(
             placed.at[:, pl.ds(step * planes, planes), :],
             turned.at[:, pl.ds(step * planes, planes), :],
-            semaphores.at[1, step, 0],
+            semaphores.at[1, step],
         )
         for step in range(steps)
     ]
+    for copy in incoming:
+        copy.start()
     for step in range(steps):
-        for copy in incoming[step]:
-            copy.start()
-    for step in range(steps):
-        for copy in incoming[step]:
-            copy.wait()
+        incoming[step].wait()
         for x in range(step * planes, (step + 1) * planes, SUB):
-            for k in range(blocks):
-                block = staged[k][x * ny : (x + SUB) * ny].reshape(SUB, ny, LANE)
-                placed[:, x : x + SUB, LANE * k : LANE * (k + 1)] = jnp.swapaxes(block, 0, 1)
+            for lane in range(0, nz, LANE):
+                block = staged[x * ny : (x + SUB) * ny, lane : lane + LANE]
+                block = jnp.swapaxes(block.reshape(SUB, ny, LANE), 0, 1)
+                placed[:, x : x + SUB, lane : lane + LANE] = block
         outgoing[step].start()
     for copy in outgoing:
         copy.wait()
@@ -164,7 +160,7 @@
 
 def turn(observed):
     slab, ny, nz = observed.shape
-    planes = SUB
+    planes = 2 * SUB if slab % (2 * SUB) == 0 else SUB
     anywhere = pl.BlockSpec(memory_space=pltpu.HBM)
     return pl.pallas_call(
         functools.partial(turn_kernel, ny, planes),
@@ -172,9 +168,9 @@
         out_specs=anywhere,
         out_shape=jax.ShapeDtypeStruct((ny, slab, nz), f32),
         scratch_shapes=[
-            [pltpu.VMEM((slab * ny, LANE), f32)] * (nz // LANE),
+            pltpu.VMEM((slab * ny, nz), f32),
             pltpu.VMEM((ny, slab, nz), f32),
-            pltpu.SemaphoreType.DMA((2, slab // planes, nz // LANE)),
+            pltpu.SemaphoreType.DMA((2, slab // planes)),
         ],
         compiler_params=pltpu.CompilerParams(vmem_limit_bytes=MOST_VMEM),
         cost_estimate=pl.CostEstimate(

time: 148 us -> 148 us (level)
  no operation moved by 1% of the time
where the time goes in v8:
time: 148 us; the launch traced here: 145 us
  blocking collectives  97.3 us (66%)
  waiting for transfers between devices  19.9 us (13%)
  Pallas kernels  19.6 us (13%)
  starting transfers between devices  6.44 us (4%)
  local copies, waits for them, and re-layouts  1.57 us (1%)
    all_to_all x3, blocking collectives, exchange(): return lax.all_to_all(blocks, 'gy', split_axis=0, concat_axis=0, tiled=True)  97.3 us
    all_to_all x1, waiting for transfers between devices, exchange(): return lax.all_to_all(blocks, 'gy', split_axis=0, concat_axis=0, tiled=True)  19.9 us
    pallas_call x2, Pallas kernels, run_passes(): pl.pallas_call(functools.partial(passes_kernel, first, last, halo, slab,...  9.11 us
    all_to_all x1, starting transfers between devices, exchange(): return lax.all_to_all(blocks, 'gy', split_axis=0, concat_axis=0, tiled=True)  6.44 us
    pallas_call x3, Pallas kernels, run_filter(): pl.pallas_call(functools.partial(filter_kernel, first, opens, closes, hal...  5.72 us
  transfers between devices with their start and end apart: 1, of which 1 were waited for; matrix products, arithmetic and copies ran while one was open for 0% of the time, Pallas kernels for 2%

profile of v8, /device:TPU:8, one launch (start us, length us, event | category | flops | bytes accessed | tf_op | source)
XLA Modules:
  0.0 145.1 jit_solution(4964930788828608905)
XLA Ops:
  0.0 2.0 %shard_map.55 = f32[16,64,256]{2,1,0:T(8,128)} custom-call(f32[1024,256]{1,0:T(8,128)} %bitcast.12), custom_call_target="tpu_custom_call" | custom-call | bytes 2097152 | tf_op jit(solution)/shard_map/pallas_call | solution.py:165
  2.0 0.0 copy-start.4
  2.1 0.0 copy-start.5
  2.1 6.4 %all-to-all-start = ((f32[16,1,64,256]{3,2,1,0:T(8,128)}), f32[16,1,64,256]{3,2,1,0:T(8,128)S(1)}, u32[]{:S(2)}, u32[]{:S(2)}) async-start(f32[16,1,64,256]{3,2,1,0:T(8,128)} %bitcast.11), calls=%async_computation | async-start | bytes 2097152 | tf_op jit(solution)/shard_map/all_to_all | solution.py:566
  8.5 0.0 copy-done.4
  8.5 0.0 copy-done.5
  8.5 0.0 copy-start
  8.5 0.1 fusion
  8.6 0.5 copy-done
  9.2 0.0 copy-start.1
  9.2 2.7 %shard_map.57.refs_1_ = f32[1024,256]{1,0:T(8,128)S(1)} custom-call(f32[16]{0:T(128)S(1)} %copy-done, bf16[256,640]{1,0:T(8,128)(2,1)S(1)} %pad.5.code_ref), custom_call_target="tpu_custom_call" | custom-call | flops 15728640000 | bytes 1048576 | tf_op jit(solution)/shard_map/pallas_call | solution.py:104
  11.9 0.0 copy-start.2
  11.9 1.0 copy-done.2
  12.9 19.9 %all-to-all-done.refs_0_ = f32[16,1,64,256]{3,2,1,0:T(8,128)S(1)} async-done(((f32[16,1,64,256]{3,2,1,0:T(8,128)}), f32[16,1,64,256]{3,2,1,0:T(8,128)S(1)}, u32[]{:S(2)}, u32[]{:S(2)}) %all-to-all-start) | async-done | bytes 1048608 | tf_op jit(solution)/shard_map/all_to_all | solution.py:566
  32.7 0.0 copy-done.1
  32.7 0.0 copy-start.3
  32.7 1.2 shard_map.56.refs_0_
  33.9 0.0 copy-done.3
  34.0 1.8 %shard_map.58 = (f32[16,1,19,8,128]{4,3,2,1,0:T(8,128)S(1)}, f32[1,1024,256]{2,1,0:T(8,128)S(1)}, f32[1024,256]{1,0:T(8,128)S(1)}) custom-call(f32[1,1024,256]{2,1,0:T(8,128)S(1)} %shard_map.56.refs_0_, f32[1024,256]{1,0:T(8,128)S(1)} %copy-done.3, bf16[2,6,256,256]{3,2,1,0:T(8,128)(2,1)S(1)} %copy-done.1), custom_call_target="tpu_custom_call" | custom-call | flops 1207959552 | bytes 2097152 | tf_op jit(solution)/shard_map/pallas_call | solution.py:294
  35.8 34.9 %all_to_all.20 = f32[16,1,19,8,128]{4,3,2,1,0:T(8,128)S(1)} all-to-all(f32[16,1,19,8,128]{4,3,2,1,0:T(8,128)S(1)} %get-tuple-element.12), channel_id=1, replica_groups=mesh['groups'=2,'gy'=16] {'gy'}, dimensions={0} | all-to-all | bytes 2490368 | tf_op jit(solution)/shard_map/all_to_all | solution.py:566
  70.7 4.2 %shard_map.59 = (f32[16,64,256]{2,1,0:T(8,128)S(1)}, f32[16,72,256]{2,1,0:T(8,128)S(1)}, f32[16,72,256]{2,1,0:T(8,128)S(1)}, f32[16,72,256]{2,1,0:T(8,128)S(1)}) custom-call(f32[16,19,8,128]{3,2,1,0:T(8,128)S(1)} %bitcast.8), custom_call_target="tpu_custom_call" | custom-call | flops 39321600 | bytes 10485760 | tf_op jit(solution)/shard_map/pallas_call | solution.py:538
  74.9 29.2 %all_to_all.21.refs_0_ = f32[16,1,64,256]{3,2,1,0:T(8,128)S(1)} all-to-all(f32[16,1,64,256]{3,2,1,0:T(8,128)S(1)} %bitcast.10), channel_id=1, replica_groups=mesh['groups'=2,'gy'=16] {'gy'}, dimensions={0} | all-to-all | bytes 2097152 | tf_op jit(solution)/shard_map/all_to_all | solution.py:566
  104.2 2.7 %shard_map.60 = f32[16,1,18,8,128]{4,3,2,1,0:T(8,128)S(1)} custom-call(f32[16,1,64,256]{3,2,1,0:T(8,128)S(1)} %all_to_all.21.refs_0_, f32[1024,256]{1,0:T(8,128)S(1)} %get-tuple-element.14.refs_1_, bf16[2,6,256,256]{3,2,1,0:T(8,128)(2,1)S(1)} %copy-done.1, f32[1,1024,256]{2,1,0:T(8,128)S(1)} %get-tuple-element.15.refs_3_), custom_call_target="tpu_custom_call" | custom-call | flops 2415919104 | bytes 2097152 | tf_op jit(solution)/shard_map/pallas_call | solution.py:294
  106.9 33.2 %all_to_all.22 = f32[16,1,18,8,128]{4,3,2,1,0:T(8,128)S(1)} all-to-all(f32[16,1,18,8,128]{4,3,2,1,0:T(8,128)S(1)} %shard_map.60), channel_id=1, replica_groups=mesh['groups'=2,'gy'=16] {'gy'}, dimensions={0} | all-to-all | bytes 2359296 | tf_op jit(solution)/shard_map/all_to_all | solution.py:566
  140.1 4.9 %shard_map.61 = f32[1024,256]{1,0:T(8,128)} custom-call(f32[16,18,8,128]{3,2,1,0:T(8,128)S(1)} %bitcast.9, f32[16,72,256]{2,1,0:T(8,128)S(1)} %get-tuple-element.16.refs_0_, f32[16,72,256]{2,1,0:T(8,128)S(1)} %get-tuple-element.17.refs_1_, f32[16,72,256]{2,1,0:T(8,128)S(1)} %get-tuple-element.18.refs_2_), custom_call_target="tpu_custom_call" | custom-call | flops 35389440 | bytes 9437184 | tf_op jit(solution)/shard_map/pallas_call | solution.py:538
  (1 shorter events, 0.0 us)
Async XLA Ops:
  2.0 6.5 %copy-start.4 = (s32[513,129]{0,1:T(8,128)S(1)}, s32[513,129]{0,1:T(8,128)}, u32[]{:S(2)}) copy-start(s32[513,129]{0,1:T(8,128)} %param.7) | copy-start | bytes 794128
  2.1 6.5 %copy-start.5 = (s32[513,129]{0,1:T(8,128)S(1)}, s32[513,129]{0,1:T(8,128)}, u32[]{:S(2)}) copy-start(s32[513,129]{0,1:T(8,128)} %param.8) | copy-start | bytes 794128
  2.1 30.7 %all-to-all-start = ((f32[16,1,64,256]{3,2,1,0:T(8,128)}), f32[16,1,64,256]{3,2,1,0:T(8,128)S(1)}, u32[]{:S(2)}, u32[]{:S(2)}) async-start(f32[16,1,64,256]{3,2,1,0:T(8,128)} %bitcast.11), calls=%async_computation | async-start | bytes 2097152 | tf_op jit(solution)/shard_map/all_to_all | solution.py:566
  8.5 0.7 copy-start
  9.2 23.6 %copy-start.1 = (bf16[2,6,256,256]{3,2,1,0:T(8,128)(2,1)S(1)}, bf16[2,6,256,256]{3,2,1,0:T(8,128)(2,1)}, u32[]{:S(2)}) copy-start(bf16[2,6,256,256]{3,2,1,0:T(8,128)(2,1)} %constant.9.clone.refs_1_.refs_2_) | copy-start | bytes 4718596
  11.9 1.0 copy-start.2
  32.7 1.2 copy-start.3
